TPU v7x, 32 devices: a whole 2x2x4 slice. The times are simulated.
32 devices in a mesh: shot: 2 (over x), strip: 16 (over z, y, core).
Axes of the slice: x: 2, y: 2, z: 4, core: 2. Of those that a mesh axis runs over, the one named last changes fastest.
Arguments:
- waves: float32 [2, 2, 8, 512, 512], P(None, None, 'shot', 'strip'), parts along dimension 2, may hold values from -6 to 6
- levels: int32 [512, 512], P('strip'), may hold values from 0 to 4
- coeffs: float32 [2, 4, 5, 17], replicated, may hold values from -0.7 to 0.7
- angles: float32 [4, 5], replicated, may hold values from -3.140625 to 3.140625
- order: int32 [8], P('shot'), parts along dimension 0, may hold values from 0 to 3, each once
Outputs:
- waves_out: float32 [2, 2, 8, 512, 512], P(None, None, 'shot', 'strip'), parts along dimension 2
- image: float32 [4, 512, 512], P('shot', 'strip'), parts along dimension 0
There are 2 independent parts, one for each index of `shot`. A program takes and returns all parts, laid end to end along the dimension named above; an argument that names none is the same for every part. Nothing has to cross between parts.
Inputs may be any that keep to these rules, and one draw needn't show every extreme that they name: order names every table row once.
All inputs are finite; a program needn't handle non-finite values.
Results may differ from a plain program's by a relative error of at most 0.00013.
Values sent between devices are 32-bit elements; how exact they have to be, the bound alone decides.
No kernel may reach another device: no remote copies, remote signals or barrier semaphores. Data moves between devices by JAX's collectives and lax.ppermute only.
A program may use at most 64 MiB of HBM per device.

v0:
```python
import functools

import jax
import jax.numpy as jnp
from jax import lax
from jax.experimental import pallas as pl
from jax.experimental.pallas import tpu as pltpu
from jax.sharding import PartitionSpec as P

STEPS = 2
LANES = 128
F32 = jnp.float32
BF16 = jnp.bfloat16


def pick(values, masks):
    out = values[0]
    for value, mask in zip(values[1:], masks):
        out = jnp.where(mask, value, out)
    return out


def level_masks(level, count):
    return [level == float(l) for l in range(1, count)]


def split(cells):
    high = cells.astype(BF16)
    return high, (cells - high.astype(F32)).astype(BF16)


def build_filters(coef_ref, order_ref, pad_ref, lhs_ref, block):
    freqs = lhs_ref.shape[1]
    levels, taps = coef_ref.shape[2:]
    pad_ref[...] = jnp.zeros_like(pad_ref)
    pad_ref[:, :, :levels, :taps] = coef_ref[...]
    wide = 2 * block
    lane = lax.broadcasted_iota(jnp.int32, (block, LANES), 1)
    early = (lane % wide) < block

    def body(f, carry):
        row = order_ref[f]
        real, imag = pad_ref[0, row], pad_ref[1, row]
        tables = (real - pltpu.roll(imag, wide, 1), imag + pltpu.roll(real, wide, 1))
        for level in range(levels):
            for part in range(2):
                line = jnp.broadcast_to(tables[part][level : level + 1], (block, LANES))
                band = pltpu.roll(line, 0, 1, stride=1, stride_axis=0)
                swapped = jnp.where(early, pltpu.roll(band, LANES - block, 1), pltpu.roll(band, block, 1))
                at = (level * 2 + part) * block
                for v, cells in enumerate((band, swapped)):
                    high, low = split(cells)
                    high = high.astype(F32)
                    lhs_ref[v, f, at : at + block, :LANES] = (high + pltpu.roll(high, 2 * wide, 1)).astype(BF16)
                    lhs_ref[v, f, at : at + block, LANES:] = low
        return carry

    lax.fori_loop(0, freqs, body, 0)


def band_product(lhs, reals, imags):
    rhs = jnp.concatenate([reals[0], imags[0], reals[1], imags[1], reals[0], imags[0]], axis=0)
    return jnp.dot(lhs[:, : rhs.shape[0]], rhs, preferred_element_type=F32)


def band_pick(found, masks, block):
    count = found.shape[0] // (2 * block)
    return [
        pick([found[(l * 2 + part) * block : (l * 2 + part + 1) * block] for l in range(count)], masks)
        for part in range(2)
    ]


def turn_tables(turn_ref, f, masks):
    height, width = masks[0].shape
    tables = []
    for part in range(2):
        values = []
        for l in range(len(masks) + 1):
            tile = turn_ref[f, part, l]
            tile = jnp.concatenate([tile] * (height // tile.shape[0]), axis=0)
            values.append(jnp.concatenate([tile] * (width // LANES), axis=1))
        tables.append(pick(values, masks))
    return tables


def rotate(cells, cosine, sine):
    real, imag = cells
    return real * cosine - imag * sine, real * sine + imag * cosine


def to_columns(fields, block):
    chunks = fields[0].shape[1] // LANES
    return jnp.concatenate(
        [field[:, c * LANES : (c + 1) * LANES] for c in range(chunks) for field in fields], axis=0
    ).T


def inline(lhs, fields, masks_t, block):
    half = block // 2
    count = len(fields)
    chunks = fields[0][0].shape[1] // LANES
    step = count * block
    lane = lax.broadcasted_iota(jnp.int32, (half, LANES), 1)
    columns = []
    for part in range(2):
        columns.append(to_columns([field[part] for field in fields], block))
        yield
    parts = []
    for cols in columns:
        before = jnp.where(lane < step, 0.0, pltpu.roll(cols[LANES - half :], step, 1))
        after = jnp.where(lane >= LANES - step, 0.0, pltpu.roll(cols[:half], LANES - step, 1))
        parts.append(split(jnp.concatenate([before, cols, after], axis=0)))
        yield
    mid = LANES // 2
    halves = [[[], []], [[], []]]
    masks_t = masks_t()
    found = []
    spots = list(range(0, mid, block))

    def finish(at):
        masks = [jnp.concatenate([m[at : at + block], m[mid + at : mid + at + block]], axis=1) for m in masks_t]
        got = band_pick(found.pop(0), masks, block)
        for part in range(2):
            halves[part][0].append(got[part][:, :LANES])
            halves[part][1].append(got[part][:, LANES:])

    for n, at in enumerate(spots):
        windows = [
            [
                jnp.concatenate([x[at : at + 2 * block], x[mid + at : mid + at + 2 * block]], axis=1)
                for x in parts[part]
            ]
            for part in range(2)
        ]
        found.append(band_product(lhs, windows[0], windows[1]))
        yield
        if n >= LAG:
            finish(spots[n - LAG])
    for at in spots[len(spots) - LAG :]:
        finish(at)
    yield
    back = []
    for part in range(2):
        back.append(jnp.concatenate(halves[part][0] + halves[part][1], axis=0).T)
        yield
    return [
        [
            jnp.concatenate(
                [back[part][(c * count + i) * block : (c * count + i + 1) * block] for c in range(chunks)], axis=1
            )
            for part in range(2)
        ]
        for i in range(count)
    ]


def split_fields(fields):
    return [list(zip(*[split(cells) for cells in field])) for field in fields]


def saved(ref, f):
    return [[[ref[f, i, kind, part] for part in range(2)] for kind in range(2)] for i in range(2)]


def save(ref, f, blocks):
    for i in range(2):
        for kind in range(2):
            for part in range(2):
                ref[f, i, kind, part] = blocks[i][kind][part]


def crossline(lhs, first, second, masks, block):
    wide = 2 * LANES
    width = first[0][0][0].shape[1]
    pieces = [[[], []], [[], []]]
    spots = [(i, at) for i in range(2) for at in range(0, width, wide)]
    found = []

    def finish(spot):
        i, at = spot
        got = band_pick(found.pop(0), [m[:, at : at + wide] for m in masks], block)
        for part in range(2):
            pieces[i][part].append(got[part])

    for n, (i, at) in enumerate(spots):
        windows = [
            [
                jnp.concatenate([b[i][kind][part][:, at : at + wide] for b in (first, second)], axis=0)
                for kind in range(2)
            ]
            for part in range(2)
        ]
        found.append(band_product(lhs, windows[0], windows[1]))
        yield
        if n >= LAG:
            finish(spots[n - LAG])
    for spot in spots[len(spots) - LAG :]:
        finish(spot)
    yield
    return [[jnp.concatenate(p, axis=1) for p in piece] for piece in pieces]


def interleave(chains, skew):
    live = dict(enumerate(chains))
    tick = 0
    while live:
        for n in list(live):
            if tick >= n * skew and next(live[n], live) is live:
                del live[n]
        tick += 1


def image_of(fields):
    (sr, si), (qr, qi) = fields
    return sr * qr - si * qi


def raw_fields(get, cosine, sine):
    fields = [[get(i, p) for p in range(2)] for i in range(2)]
    fields[1][1] = -fields[1][1]
    return [rotate(field, cosine, sine) for field in fields]


def put_done(done_ref, f, fields):
    (sr, si), (qr, qi) = fields
    done_ref[0, 0, f], done_ref[0, 1, f], done_ref[1, 0, f], done_ref[1, 1, f] = sr, si, qr, -qi


def window_levels(ref, inner, outer, inner_at, block):
    ref[pl.ds(pl.multiple_of(inner_at, block), block)] = inner
    ref[pl.ds(pl.multiple_of(block - inner_at, block), block)] = outer
    return ref[block // 2 : block // 2 + block]


def first_kernel(
    order_ref, cs_ref, coef_ref, waves_ref, lev_ref, fast_ref, halo_ref,
    out_ref, img_ref, edge_ref, mid_ref, lhs_ref, turn_ref,
    pad_ref, levw_ref, levt_ref, done_ref, acc_ref, sem,
):
    freqs = lhs_ref.shape[1]
    levels, taps = coef_ref.shape[2:]
    block = taps - 1
    half = block // 2
    rows = lev_ref.shape[0]
    c = lax.axis_index("strip") % 2
    for f in range(freqs):
        for part in range(2):
            for l in range(levels):
                turn_ref[f, part, l] = jnp.full(turn_ref.shape[3:], cs_ref[part, order_ref[f], l], F32)
    build_filters(coef_ref, order_ref, pad_ref, lhs_ref, block)
    slow_row = pl.multiple_of(block * c, block)
    fast_row = pl.multiple_of(block * (1 - c), block)
    lev_slow = lev_ref[pl.ds(slow_row, block)].astype(F32)
    lev_fast = lev_ref[pl.ds(fast_row, block)].astype(F32)
    lev_halo = halo_ref[...].astype(F32)
    lev_mid = lev_ref[half : half + block].astype(F32)
    lev_edge = window_levels(levw_ref, lev_fast, lev_halo, block * c, block)
    blocks = (lev_slow, lev_fast, lev_halo, lev_mid, lev_edge)
    for slot, lev in enumerate(blocks):
        levt_ref[slot] = to_columns([lev, lev], block)
    masks = [level_masks(lev, levels) for lev in blocks]
    acc_ref[...] = jnp.zeros_like(acc_ref)
    copies = []
    ready = {}

    def start_chain(f, slot):
        cosine, sine = turn_tables(turn_ref, f, masks[slot])
        if slot < 2:
            at = (slow_row, fast_row)[slot]
            get = lambda i, p: waves_ref[i, p, f, pl.ds(at, block)]
        else:
            get = lambda i, p: fast_ref[(i * 2 + p) * freqs + f]
        fields = raw_fields(get, cosine, sine)
        yield
        fields = yield from inline(lhs_ref[0, f], fields, lambda: level_masks(levt_ref[slot], levels), block)
        ready[f, slot] = split_fields(fields)
        if slot == 0:
            save(edge_ref, f, ready[f, slot])

    def next_chain(f, slot):
        first, second = ((0, 1), (1, 2))[slot]
        fields = yield from crossline(lhs_ref[c, f], ready[f, first], ready[f, second], masks[3 + slot], block)
        acc_ref[slot] += image_of(fields)
        cosine, sine = turn_tables(turn_ref, f, masks[3 + slot])
        fields = [rotate(field, cosine, sine) for field in fields]
        yield
        fields = yield from inline(lhs_ref[0, f], fields, lambda: level_masks(levt_ref[3 + slot], levels), block)
        ready[f, 3 + slot] = split_fields(fields)
        if slot == 0:
            save(mid_ref, f, ready[f, 3])

    def last_chain(f):
        fields = yield from crossline(lhs_ref[c, f], ready[f, 3], ready[f, 4], masks[1], block)
        acc_ref[2] += image_of(fields)
        put_done(done_ref, f, fields)
        copies.append(
            pltpu.make_async_copy(done_ref.at[:, :, f], out_ref.at[:, :, f, pl.ds(fast_row, block)], sem.at[f])
        )
        copies[-1].start()

    interleave([start_chain(f, slot) for f in range(freqs) for slot in range(3)], SKEW1)
    interleave([next_chain(f, slot) for f in range(freqs) for slot in range(2)], SKEW1)
    copies.append(pltpu.make_async_copy(acc_ref.at[0], img_ref.at[0, pl.ds(half, block)], sem.at[freqs]))
    own_row = pl.multiple_of(half * c, half)
    edge_row = pl.multiple_of((rows - half) * (1 - c), half)
    copies.append(
        pltpu.make_async_copy(
            acc_ref.at[1, pl.ds(own_row, half)], img_ref.at[0, pl.ds(edge_row, half)], sem.at[freqs + 1]
        )
    )
    for copy in copies:
        copy.start()
    interleave([last_chain(f) for f in range(freqs)], SKEW1)
    copies.append(pltpu.make_async_copy(acc_ref.at[2], img_ref.at[1, pl.ds(fast_row, block)], sem.at[freqs + 2]))
    copies[-1].start()
    for copy in copies:
        copy.wait()


def second_kernel(
    offset, first, last,
    slow_ref, halo_ref, lev_ref, lhs_ref, turn_ref, edge_ref, mid_ref, *refs,
):
    if first:
        sum_in_ref = None
        waves_ref, img_in_ref, out_ref, img_ref, sum_ref, levw_ref, levt_ref, done_ref, sem = refs
    else:
        sum_in_ref, waves_ref, img_in_ref, out_ref, img_ref, sum_ref, levw_ref, levt_ref, done_ref, sem = refs
    del img_in_ref
    del waves_ref
    levels = turn_ref.shape[2]
    block = lhs_ref.shape[2] // (2 * levels)
    group = done_ref.shape[2]
    half = block // 2
    rows = lev_ref.shape[0]
    index = lax.axis_index("strip")
    c = index % 2
    outside = jnp.where(c == 0, index == 0, index == lax.axis_size("strip") - 1)
    inside = jnp.where(outside, 0.0, 1.0).astype(F32)
    slow_row = pl.multiple_of(block * c, block)
    lev_near = lev_ref[pl.ds(slow_row, block)].astype(F32)
    lev_halo = halo_ref[...].astype(F32)
    lev_edge = window_levels(levw_ref, lev_near, lev_halo, block * (1 - c), block)
    for slot, lev in enumerate((lev_halo, lev_edge)):
        levt_ref[slot] = to_columns([lev, lev], block)
    masks_near, masks_halo, masks_edge = [level_masks(lev, levels) for lev in (lev_near, lev_halo, lev_edge)]
    line = lax.broadcasted_iota(jnp.int32, lev_edge.shape, 0)
    keep = jnp.where((line >= half) == (c == 0), 1.0, inside)
    sum_ref[...] = jnp.zeros_like(sum_ref) if first else sum_in_ref[...]
    copies = []

    def chain(g):
        f = offset + g
        cosine, sine = [inside * t for t in turn_tables(turn_ref, f, masks_halo)]
        get = lambda i, p: slow_ref[(i * 2 + p) * group + g]
        fields = raw_fields(get, cosine, sine)
        yield
        fields = yield from inline(lhs_ref[0, f], fields, lambda: level_masks(levt_ref[0], levels), block)
        outer = split_fields(fields)
        yield
        fields = yield from crossline(lhs_ref[1 - c, f], saved(edge_ref, f), outer, masks_edge, block)
        sum_ref[0] += image_of(fields)
        cosine, sine = [keep * t for t in turn_tables(turn_ref, f, masks_edge)]
        fields = [rotate(field, cosine, sine) for field in fields]
        yield
        if last and g == group - 1:
            own_row = pl.multiple_of(half * (1 - c), half)
            edge_row = pl.multiple_of((rows - half) * c, half)
            copies.append(
                pltpu.make_async_copy(
                    sum_ref.at[0, pl.ds(own_row, half)], img_ref.at[0, pl.ds(edge_row, half)], sem.at[group]
                )
            )
            copies[-1].start()
        fields = yield from inline(lhs_ref[0, f], fields, lambda: level_masks(levt_ref[1], levels), block)
        outer = split_fields(fields)
        yield
        fields = yield from crossline(lhs_ref[1 - c, f], saved(mid_ref, f), outer, masks_near, block)
        sum_ref[1] += image_of(fields)
        put_done(done_ref, g, fields)
        copies.append(
            pltpu.make_async_copy(done_ref.at[:, :, g], out_ref.at[:, :, f, pl.ds(slow_row, block)], sem.at[g])
        )
        copies[-1].start()

    interleave([chain(g) for g in range(group)], SKEW)
    if last:
        copies.append(
            pltpu.make_async_copy(sum_ref.at[1], img_ref.at[1, pl.ds(slow_row, block)], sem.at[group + 1])
        )
        copies[-1].start()
    for copy in copies:
        copy.wait()


VMEM = pl.BlockSpec(memory_space=pltpu.VMEM)
SMEM = pl.BlockSpec(memory_space=pltpu.SMEM)
ANY = pl.BlockSpec(memory_space=pl.ANY)
LIMIT = 48 * 1024 * 1024
SKEW = 3
SKEW1 = 2
LAG = 1
GROUPS = 1


def on_device(waves, levels, coeffs, angles, order):
    freqs = order.shape[0]
    rows, width = levels.shape
    level_count, taps = coeffs.shape[2:]
    block = taps - 1
    count = lax.axis_size("strip")
    index = lax.axis_index("strip")
    c = index % 2
    groups = GROUPS if freqs % GROUPS == 0 else 1
    group = freqs // groups

    def side(cells, start, low=0, high=freqs):
        cells = lax.dynamic_slice_in_dim(cells, start, block, axis=3)
        return cells[:, :, low:high].reshape(-1, block, width)

    shots = lax.axis_size("shot")
    across, within = [], []
    for shot in range(shots):
        for i in range(count):
            j = i + 1 if i % 2 else i - 1
            other = shot if 0 <= j < count else min(shot ^ 1, shots - 1)
            across.append((shot * count + i, other * count + (j if 0 <= j < count else i)))
            within.append((shot * count + i, shot * count + (i ^ 1)))
    axes = ("shot", "strip")

    slow_row, fast_row = c * (rows - block), (1 - c) * (rows - block)
    slow = [lax.ppermute(side(waves, slow_row, 0, group), axes, across)]
    fast = lax.ppermute(side(waves, fast_row), axes, within)
    cells, marks, fast = lax.optimization_barrier((waves, levels, fast))
    fast_levels = lax.ppermute(lax.dynamic_slice_in_dim(marks, fast_row, block, axis=0), axes, within)
    slow_levels = lax.ppermute(lax.dynamic_slice_in_dim(marks, slow_row, block, axis=0), axes, across)
    for g in range(1, groups):
        slow.append(lax.ppermute(side(cells, slow_row, g * group, (g + 1) * group), axes, across))

    turns = jnp.stack([jnp.cos(angles), jnp.sin(angles)])
    lhs_shape = (2, freqs, 2 * level_count * block, 2 * LANES)
    state = (freqs, 2, 2, 2, block, width)
    dots = 16 * freqs * 2 * lhs_shape[2] * 12 * block * width
    waves_out, image, edge, middle, lhs, tiles = pl.pallas_call(
        first_kernel,
        out_shape=[
            jax.ShapeDtypeStruct(waves.shape, F32),
            jax.ShapeDtypeStruct((STEPS, rows, width), F32),
            jax.ShapeDtypeStruct(state, BF16),
            jax.ShapeDtypeStruct(state, BF16),
            jax.ShapeDtypeStruct(lhs_shape, BF16),
            jax.ShapeDtypeStruct((freqs, 2, level_count, 8, LANES), F32),
        ],
        in_specs=[SMEM, SMEM, VMEM, VMEM, VMEM, VMEM, VMEM],
        out_specs=[ANY, ANY, VMEM, VMEM, VMEM, VMEM],
        scratch_shapes=[
            pltpu.VMEM(coeffs.shape[:2] + (8, LANES), F32),
            pltpu.VMEM((2 * block, width), F32),
            pltpu.VMEM((5, LANES, LANES), F32),
            pltpu.VMEM((2, 2, freqs, block, width), F32),
            pltpu.VMEM((3, block, width), F32),
            pltpu.SemaphoreType.DMA((freqs + 3,)),
        ],
        compiler_params=pltpu.CompilerParams(vmem_limit_bytes=LIMIT),
        cost_estimate=pl.CostEstimate(flops=2 * dots, bytes_accessed=8 << 20, transcendentals=0),
        name="own_rows",
    )(order, turns, coeffs, waves, levels, fast, fast_levels)
    total = []
    for g in range(groups):
        aliased = 7 + len(total)
        waves_out, image, *total = pl.pallas_call(
            functools.partial(second_kernel, g * group, g == 0, g == groups - 1),
            out_shape=[
                jax.ShapeDtypeStruct(waves.shape, F32),
                jax.ShapeDtypeStruct((STEPS, rows, width), F32),
                jax.ShapeDtypeStruct((STEPS, block, width), F32),
            ],
            in_specs=[VMEM] * aliased + [ANY, ANY],
            out_specs=[ANY, ANY, VMEM],
            scratch_shapes=[
                pltpu.VMEM((2 * block, width), F32),
                pltpu.VMEM((2, LANES, LANES), F32),
                pltpu.VMEM((2, 2, group, block, width), F32),
                pltpu.SemaphoreType.DMA((group + 2,)),
            ],
            input_output_aliases={aliased: 0, aliased + 1: 1},
            compiler_params=pltpu.CompilerParams(vmem_limit_bytes=LIMIT),
            cost_estimate=pl.CostEstimate(flops=dots // groups, bytes_accessed=4 << 20, transcendentals=0),
            name=f"edge_rows_{g}",
        )(slow[g], slow_levels, levels, lhs, tiles, edge, middle, *total, waves_out, image)
    return waves_out, image


def solution(mesh):
    in_specs = (P(None, None, "shot", "strip", None), P("strip", None), P(), P(), P("shot"))
    out_specs = (P(None, None, "shot", "strip", None), P("shot", "strip", None))
    return jax.shard_map(
        on_device, mesh=mesh, in_specs=in_specs, out_specs=out_specs, check_vma=False
    )
```

profile of v0, /device:TPU:9, one launch (start us, length us, event | category | flops | bytes accessed | tf_op | source)
XLA Modules:
  0.0 21.4 jit_solution(13459816207864850070)
XLA Ops:
  0.7 0.0 copy-start.1
  0.7 0.0 copy-start
  0.7 1.4 %constant_dynamic-slice_fusion.2 = (f32[2,2,4,16,512]{4,3,2,1,0:T(8,128)S(1)}, f32[2,2,4,16,512]{4,3,2,1,0:T(8,128)S(1)}) fusion(f32[2,2,4,32,512]{4,3,2,1,0:T(8,128)} %waves_ref.1, s32[]{:T(128)S(6)} %select_n.17, s32[]{:T(128)S(6)} %select_n.16), kind=kLoop, calls=%fused_computation.5 | loop fusion | bytes 2097160 | tf_op jit(solution)/shard_map/dynamic_slice | solution.py:419
  2.0 0.0 copy-start.4
  2.1 0.7 %collective-permute-start.1 = (f32[16,16,512]{2,1,0:T(8,128)S(1)}, f32[16,16,512]{2,1,0:T(8,128)S(1)}, u32[]{:S(2)}, u32[]{:S(2)}) collective-permute-start(f32[16,16,512]{2,1,0:T(8,128)S(1)} %bitcast.7), channel_id=1, source_target_pairs={{0,1},{1,0},{2,3},{3,2},{4,5},{5,4},{6,7},{7,6},{8,9},{9,8},{10,11... | collective-permute-start | bytes 1572872 | tf_op jit(solution)/shard_map/ppermute | solution.py:434
  2.8 1.2 %collective-permute-start = (f32[16,16,512]{2,1,0:T(8,128)S(1)}, f32[16,16,512]{2,1,0:T(8,128)S(1)}, u32[]{:S(2)}, u32[]{:S(2)}) collective-permute-start(f32[16,16,512]{2,1,0:T(8,128)S(1)} %bitcast.6), channel_id=1, source_target_pairs={{0,16},{1,2},{2,1},{3,4},{4,3},{5,6},{6,5},{7,8},{8,7},{9,10},{10,... | collective-permute-start | bytes 1572872 | tf_op jit(solution)/shard_map/ppermute | solution.py:433
  4.0 0.0 copy-done.4
  4.0 0.3 %collective-permute-done.1.fast_ref = f32[16,16,512]{2,1,0:T(8,128)S(1)} collective-permute-done((f32[16,16,512]{2,1,0:T(8,128)S(1)}, f32[16,16,512]{2,1,0:T(8,128)S(1)}, u32[]{:S(2)}, u32[]{:S(2)}) %collective-permute-start.1) | collective-permute-done | bytes 524320 | tf_op jit(solution)/shard_map/ppermute | solution.py:434
  4.3 0.0 copy-done.1
  4.3 0.0 copy-start.3
  4.3 0.4 %collective-permute-start.3 = (s32[16,512]{1,0:T(8,128)S(1)}, s32[16,512]{1,0:T(8,128)S(1)}, u32[]{:S(2)}, u32[]{:S(2)}) collective-permute-start(s32[16,512]{1,0:T(8,128)S(1)} %get-tuple-element.24), channel_id=1, source_target_pairs={{0,1},{1,0},{2,3},{3,2},{4,5},{5,4},{6,7},{7,6},{8,9},{9,8},{10,11... | collective-permute-start | bytes 98312 | tf_op jit(solution)/shard_map/ppermute | solution.py:436
  4.8 0.3 %copy-done.3 = f32[2,4,5,17]{3,1,2,0:T(4,128)S(1)} copy-done((f32[2,4,5,17]{3,1,2,0:T(4,128)S(1)}, f32[2,4,5,17]{3,1,2,0:T(4,128)}, u32[]{:S(2)}) %copy-start.3) | copy-done | bytes 2744
  5.1 0.0 copy-start.2
  5.1 1.5 %collective-permute-start.2 = (s32[16,512]{1,0:T(8,128)S(1)}, s32[16,512]{1,0:T(8,128)S(1)}, u32[]{:S(2)}, u32[]{:S(2)}) collective-permute-start(s32[16,512]{1,0:T(8,128)S(1)} %get-tuple-element.25), channel_id=1, source_target_pairs={{0,16},{1,2},{2,1},{3,4},{4,3},{5,6},{6,5},{7,8},{8,7},{9,10},{10,... | collective-permute-start | bytes 98312 | tf_op jit(solution)/shard_map/ppermute | solution.py:437
  6.6 0.0 collective-permute-done.3.halo_ref
  6.6 0.0 copy-done
  6.6 0.0 copy-done.2
  6.6 7.5 %own_rows.1 = (f32[2,2,4,32,512]{4,3,2,1,0:T(8,128)}, f32[2,32,512]{2,1,0:T(8,128)}, bf16[4,2,2,2,16,512]{5,4,3,2,1,0:T(8,128)(2,1)S(1)}, bf16[4,2,2,2,16,512]{5...) custom-call(s32[4]{0:T(128)S(1)} %copy-done.2, ...), custom_call_target="tpu_custom_call" | custom-call | flops 4026531840 | bytes 8388608 | tf_op jit(solution)/shard_map/own_rows/pallas_call | solution.py:445
  14.0 3.3 %collective-permute-done.slow_ref = f32[16,16,512]{2,1,0:T(8,128)S(1)} collective-permute-done((f32[16,16,512]{2,1,0:T(8,128)S(1)}, f32[16,16,512]{2,1,0:T(8,128)S(1)}, u32[]{:S(2)}, u32[]{:S(2)}) %collective-permute-start) | collective-permute-done | bytes 524320 | tf_op jit(solution)/shard_map/ppermute | solution.py:433
  17.4 0.4 %collective-permute-done.2.halo_ref = s32[16,512]{1,0:T(8,128)S(1)} collective-permute-done((s32[16,512]{1,0:T(8,128)S(1)}, s32[16,512]{1,0:T(8,128)S(1)}, u32[]{:S(2)}, u32[]{:S(2)}) %collective-permute-start.2) | collective-permute-done | bytes 32800 | tf_op jit(solution)/shard_map/ppermute | solution.py:437
  17.7 3.7 %edge_rows_0.1 = (f32[2,2,4,32,512]{4,3,2,1,0:T(8,128)}, f32[2,32,512]{2,1,0:T(8,128)}, f32[2,16,512]{2,1,0:T(8,128)}) custom-call(f32[16,16,512]{2,1,0:T(8,128)S(1)} %collective-permute-done.slow_ref, s32[16,512]{1,0:T(8,128)S(1)} %collective-permute-done.2.halo_ref, s32[32,512]{1,0:T(8,128)S(1)} %copy-done.1, ...), custom_call_target="tpu_custom_call", output_to_operand_aliasing={{0}: (7, {}), {1}: (8, {})} | custom-call | flops 2013265920 | bytes 4194304 | tf_op jit(solution)/shard_map/edge_rows_0/pallas_call | solution.py:472
  (4 shorter events, 0.1 us)
Async XLA Ops:
  0.7 3.7 %copy-start.1 = (s32[32,512]{1,0:T(8,128)S(1)}, s32[32,512]{1,0:T(8,128)}, u32[]{:S(2)}) copy-start(s32[32,512]{1,0:T(8,128)} %lev_ref.3) | copy-start | bytes 196612
  0.7 5.9 %copy-start = (f32[2,2,4,32,512]{4,3,2,1,0:T(8,128)S(1)}, f32[2,2,4,32,512]{4,3,2,1,0:T(8,128)}, u32[]{:S(2)}) copy-start(f32[2,2,4,32,512]{4,3,2,1,0:T(8,128)} %waves_ref.1) | copy-start | bytes 3145732
  2.0 2.0 %copy-start.4 = (f32[4,5]{1,0:T(4,128)S(1)}, f32[4,5]{1,0:T(4,128)}, u32[]{:S(2)}) copy-start(f32[4,5]{1,0:T(4,128)} %param.8) | copy-start | bytes 244
  2.1 2.3 %collective-permute-start.1 = (f32[16,16,512]{2,1,0:T(8,128)S(1)}, f32[16,16,512]{2,1,0:T(8,128)S(1)}, u32[]{:S(2)}, u32[]{:S(2)}) collective-permute-start(f32[16,16,512]{2,1,0:T(8,128)S(1)} %bitcast.7), channel_id=1, source_target_pairs={{0,1},{1,0},{2,3},{3,2},{4,5},{5,4},{6,7},{7,6},{8,9},{9,8},{10,11... | collective-permute-start | bytes 1572872 | tf_op jit(solution)/shard_map/ppermute | solution.py:434
  2.8 14.6 %collective-permute-start = (f32[16,16,512]{2,1,0:T(8,128)S(1)}, f32[16,16,512]{2,1,0:T(8,128)S(1)}, u32[]{:S(2)}, u32[]{:S(2)}) collective-permute-start(f32[16,16,512]{2,1,0:T(8,128)S(1)} %bitcast.6), channel_id=1, source_target_pairs={{0,16},{1,2},{2,1},{3,4},{4,3},{5,6},{6,5},{7,8},{8,7},{9,10},{10,... | collective-permute-start | bytes 1572872 | tf_op jit(solution)/shard_map/ppermute | solution.py:433
  4.3 0.7 %copy-start.3 = (f32[2,4,5,17]{3,1,2,0:T(4,128)S(1)}, f32[2,4,5,17]{3,1,2,0:T(4,128)}, u32[]{:S(2)}) copy-start(f32[2,4,5,17]{3,1,2,0:T(4,128)} %param.7) | copy-start | bytes 8164
  4.3 2.2 %collective-permute-start.3 = (s32[16,512]{1,0:T(8,128)S(1)}, s32[16,512]{1,0:T(8,128)S(1)}, u32[]{:S(2)}, u32[]{:S(2)}) collective-permute-start(s32[16,512]{1,0:T(8,128)S(1)} %get-tuple-element.24), channel_id=1, source_target_pairs={{0,1},{1,0},{2,3},{3,2},{4,5},{5,4},{6,7},{7,6},{8,9},{9,8},{10,11... | collective-permute-start | bytes 98312 | tf_op jit(solution)/shard_map/ppermute | solution.py:436
  5.1 1.5 %copy-start.2 = (s32[4]{0:T(128)S(1)}, s32[4]{0:T(128)}, u32[]{:S(2)}) copy-start(s32[4]{0:T(128)} %order_ref.1) | copy-start | bytes 52
  5.1 12.7 %collective-permute-start.2 = (s32[16,512]{1,0:T(8,128)S(1)}, s32[16,512]{1,0:T(8,128)S(1)}, u32[]{:S(2)}, u32[]{:S(2)}) collective-permute-start(s32[16,512]{1,0:T(8,128)S(1)} %get-tuple-element.25), channel_id=1, source_target_pairs={{0,16},{1,2},{2,1},{3,4},{4,3},{5,6},{6,5},{7,8},{8,7},{9,10},{10,... | collective-permute-start | bytes 98312 | tf_op jit(solution)/shard_map/ppermute | solution.py:437
where the time goes:
time: 21.6 us; the launch traced here: 21.4 us
  Pallas kernels  11.1 us (51%)
  waiting for transfers between devices  3.97 us (18%)
  starting transfers between devices  3.88 us (18%)
  local copies, waits for them, and re-layouts  1.71 us (8%)
  between operations  0.7 us (3%)
    pallas_call x1, Pallas kernels, on_device(): pl.pallas_call(first_kernel, out_shape=[jax.ShapeDtypeStruct(waves.shape,...  7.46 us
    pallas_call x1, Pallas kernels, on_device(): pl.pallas_call(functools.partial(second_kernel, g * group, g == 0, g == g...  3.69 us
    ppermute x1, waiting for transfers between devices, on_device(): slow = [lax.ppermute(side(waves, slow_row, 0, group), axes, across)]  3.32 us
    ppermute x1, starting transfers between devices, on_device(): lax.ppermute(lax.dynamic_slice_in_dim(marks, slow_row, block, axis=0), ax...  1.5 us
    dynamic_slice x1, local copies, waits for them, and re-layouts, side(): cells = lax.dynamic_slice_in_dim(cells, start, block, axis=3)  1.37 us
    ppermute x1, starting transfers between devices, on_device(): slow = [lax.ppermute(side(waves, slow_row, 0, group), axes, across)]  1.2 us
    ppermute x1, starting transfers between devices, on_device(): fast = lax.ppermute(side(waves, fast_row), axes, within)  0.74 us
    ppermute x1, starting transfers between devices, on_device(): lax.ppermute(lax.dynamic_slice_in_dim(marks, fast_row, block, axis=0), ax...  0.44 us
  transfers between devices with their start and end apart: 4, of which 3 were waited for; matrix products, arithmetic and copies ran while one was open for 0% of the time, Pallas kernels for 35%

commit v1 on v0

--- a/solution.py
+++ b/solution.py
@@ -55,7 +55,8 @@
                     lhs_ref[v, f, at : at + block, LANES:] = low
         return carry
 
-    lax.fori_loop(0, freqs, body, 0)
+    for f in range(freqs):
+        body(f, 0)
 
 
 def band_product(lhs, reals, imags):
@@ -235,14 +236,13 @@
 
 def first_kernel(
     order_ref, cs_ref, coef_ref, waves_ref, lev_ref, fast_ref, halo_ref,
-    out_ref, img_ref, edge_ref, mid_ref, lhs_ref, turn_ref,
-    pad_ref, levw_ref, levt_ref, done_ref, acc_ref, sem,
+    done_ref, acc_ref, edge_ref, mid_ref, lhs_ref, turn_ref,
+    pad_ref, levw_ref, levt_ref,
 ):
     freqs = lhs_ref.shape[1]
     levels, taps = coef_ref.shape[2:]
     block = taps - 1
     half = block // 2
-    rows = lev_ref.shape[0]
     c = lax.axis_index("strip") % 2
     for f in range(freqs):
         for part in range(2):
@@ -261,7 +261,6 @@
         levt_ref[slot] = to_columns([lev, lev], block)
     masks = [level_masks(lev, levels) for lev in blocks]
     acc_ref[...] = jnp.zeros_like(acc_ref)
-    copies = []
     ready = {}
 
     def start_chain(f, slot):
@@ -294,41 +293,23 @@
         fields = yield from crossline(lhs_ref[c, f], ready[f, 3], ready[f, 4], masks[1], block)
         acc_ref[2] += image_of(fields)
         put_done(done_ref, f, fields)
-        copies.append(
-            pltpu.make_async_copy(done_ref.at[:, :, f], out_ref.at[:, :, f, pl.ds(fast_row, block)], sem.at[f])
-        )
-        copies[-1].start()
 
     interleave([start_chain(f, slot) for f in range(freqs) for slot in range(3)], SKEW1)
     interleave([next_chain(f, slot) for f in range(freqs) for slot in range(2)], SKEW1)
-    copies.append(pltpu.make_async_copy(acc_ref.at[0], img_ref.at[0, pl.ds(half, block)], sem.at[freqs]))
-    own_row = pl.multiple_of(half * c, half)
-    edge_row = pl.multiple_of((rows - half) * (1 - c), half)
-    copies.append(
-        pltpu.make_async_copy(
-            acc_ref.at[1, pl.ds(own_row, half)], img_ref.at[0, pl.ds(edge_row, half)], sem.at[freqs + 1]
-        )
-    )
-    for copy in copies:
-        copy.start()
     interleave([last_chain(f) for f in range(freqs)], SKEW1)
-    copies.append(pltpu.make_async_copy(acc_ref.at[2], img_ref.at[1, pl.ds(fast_row, block)], sem.at[freqs + 2]))
-    copies[-1].start()
-    for copy in copies:
-        copy.wait()
 
 
 def second_kernel(
     offset, first, last,
     slow_ref, halo_ref, lev_ref, lhs_ref, turn_ref, edge_ref, mid_ref, *refs,
 ):
-    if first:
-        sum_in_ref = None
-        waves_ref, img_in_ref, out_ref, img_ref, sum_ref, levw_ref, levt_ref, done_ref, sem = refs
+    refs = list(refs)
+    sum_in_ref = None if first else refs.pop(0)
+    if last:
+        out_ref, img_ref, sum_ref, done_ref, levw_ref, levt_ref, sem = refs[-7:]
+        own_ref, own_sum_ref, *before = refs[:-7]
     else:
-        sum_in_ref, waves_ref, img_in_ref, out_ref, img_ref, sum_ref, levw_ref, levt_ref, done_ref, sem = refs
-    del img_in_ref
-    del waves_ref
+        sum_ref, done_ref, levw_ref, levt_ref = refs
     levels = turn_ref.shape[2]
     block = lhs_ref.shape[2] // (2 * levels)
     group = done_ref.shape[2]
@@ -350,6 +331,21 @@
     sum_ref[...] = jnp.zeros_like(sum_ref) if first else sum_in_ref[...]
     copies = []
 
+    def send(source, target):
+        copies.append(pltpu.make_async_copy(source, target, sem.at[len(copies)]))
+        copies[-1].start()
+
+    if last:
+        fast_row = pl.multiple_of(block * (1 - c), block)
+        own_half = pl.ds(pl.multiple_of(half * c, half), half)
+        own_edge = pl.ds(pl.multiple_of((rows - half) * (1 - c), half), half)
+        send(own_ref, out_ref.at[:, :, :, pl.ds(fast_row, block)])
+        for n, ref in enumerate(before):
+            send(ref, out_ref.at[:, :, pl.ds(n * group, group), pl.ds(slow_row, block)])
+        send(own_sum_ref.at[0], img_ref.at[0, pl.ds(half, block)])
+        send(own_sum_ref.at[1, own_half], img_ref.at[0, own_edge])
+        send(own_sum_ref.at[2], img_ref.at[1, pl.ds(fast_row, block)])
+
     def chain(g):
         f = offset + g
         cosine, sine = [inside * t for t in turn_tables(turn_ref, f, masks_halo)]
@@ -367,29 +363,19 @@
         if last and g == group - 1:
             own_row = pl.multiple_of(half * (1 - c), half)
             edge_row = pl.multiple_of((rows - half) * c, half)
-            copies.append(
-                pltpu.make_async_copy(
-                    sum_ref.at[0, pl.ds(own_row, half)], img_ref.at[0, pl.ds(edge_row, half)], sem.at[group]
-                )
-            )
-            copies[-1].start()
+            send(sum_ref.at[0, pl.ds(own_row, half)], img_ref.at[0, pl.ds(edge_row, half)])
         fields = yield from inline(lhs_ref[0, f], fields, lambda: level_masks(levt_ref[1], levels), block)
         outer = split_fields(fields)
         yield
         fields = yield from crossline(lhs_ref[1 - c, f], saved(mid_ref, f), outer, masks_near, block)
         sum_ref[1] += image_of(fields)
         put_done(done_ref, g, fields)
-        copies.append(
-            pltpu.make_async_copy(done_ref.at[:, :, g], out_ref.at[:, :, f, pl.ds(slow_row, block)], sem.at[g])
-        )
-        copies[-1].start()
+        if last:
+            send(done_ref.at[:, :, g], out_ref.at[:, :, f, pl.ds(slow_row, block)])
 
     interleave([chain(g) for g in range(group)], SKEW)
     if last:
-        copies.append(
-            pltpu.make_async_copy(sum_ref.at[1], img_ref.at[1, pl.ds(slow_row, block)], sem.at[group + 1])
-        )
-        copies[-1].start()
+        send(sum_ref.at[1], img_ref.at[1, pl.ds(slow_row, block)])
     for copy in copies:
         copy.wait()
 
@@ -401,7 +387,7 @@
 SKEW = 3
 SKEW1 = 2
 LAG = 1
-GROUPS = 1
+GROUPS = 2
 
 
 def on_device(waves, levels, coeffs, angles, order):
@@ -431,8 +417,9 @@
 
     slow_row, fast_row = c * (rows - block), (1 - c) * (rows - block)
     slow = [lax.ppermute(side(waves, slow_row, 0, group), axes, across)]
-    fast = lax.ppermute(side(waves, fast_row), axes, within)
-    cells, marks, fast = lax.optimization_barrier((waves, levels, fast))
+    near = side(waves, fast_row)
+    fast = lax.ppermute(near, axes, within)
+    cells, marks, _ = lax.optimization_barrier((waves, levels, near))
     fast_levels = lax.ppermute(lax.dynamic_slice_in_dim(marks, fast_row, block, axis=0), axes, within)
     slow_levels = lax.ppermute(lax.dynamic_slice_in_dim(marks, slow_row, block, axis=0), axes, across)
     for g in range(1, groups):
@@ -442,54 +429,52 @@
     lhs_shape = (2, freqs, 2 * level_count * block, 2 * LANES)
     state = (freqs, 2, 2, 2, block, width)
     dots = 16 * freqs * 2 * lhs_shape[2] * 12 * block * width
-    waves_out, image, edge, middle, lhs, tiles = pl.pallas_call(
+    own_done, own_sum, edge, middle, lhs, tiles = pl.pallas_call(
         first_kernel,
         out_shape=[
-            jax.ShapeDtypeStruct(waves.shape, F32),
-            jax.ShapeDtypeStruct((STEPS, rows, width), F32),
+            jax.ShapeDtypeStruct((2, 2, freqs, block, width), F32),
+            jax.ShapeDtypeStruct((3, block, width), F32),
             jax.ShapeDtypeStruct(state, BF16),
             jax.ShapeDtypeStruct(state, BF16),
             jax.ShapeDtypeStruct(lhs_shape, BF16),
             jax.ShapeDtypeStruct((freqs, 2, level_count, 8, LANES), F32),
         ],
         in_specs=[SMEM, SMEM, VMEM, VMEM, VMEM, VMEM, VMEM],
-        out_specs=[ANY, ANY, VMEM, VMEM, VMEM, VMEM],
+        out_specs=[VMEM] * 6,
         scratch_shapes=[
             pltpu.VMEM(coeffs.shape[:2] + (8, LANES), F32),
             pltpu.VMEM((2 * block, width), F32),
             pltpu.VMEM((5, LANES, LANES), F32),
-            pltpu.VMEM((2, 2, freqs, block, width), F32),
-            pltpu.VMEM((3, block, width), F32),
-            pltpu.SemaphoreType.DMA((freqs + 3,)),
         ],
         compiler_params=pltpu.CompilerParams(vmem_limit_bytes=LIMIT),
         cost_estimate=pl.CostEstimate(flops=2 * dots, bytes_accessed=8 << 20, transcendentals=0),
         name="own_rows",
     )(order, turns, coeffs, waves, levels, fast, fast_levels)
-    total = []
+    total, parts = [], []
     for g in range(groups):
-        aliased = 7 + len(total)
-        waves_out, image, *total = pl.pallas_call(
-            functools.partial(second_kernel, g * group, g == 0, g == groups - 1),
-            out_shape=[
-                jax.ShapeDtypeStruct(waves.shape, F32),
-                jax.ShapeDtypeStruct((STEPS, rows, width), F32),
-                jax.ShapeDtypeStruct((STEPS, block, width), F32),
-            ],
-            in_specs=[VMEM] * aliased + [ANY, ANY],
-            out_specs=[ANY, ANY, VMEM],
-            scratch_shapes=[
-                pltpu.VMEM((2 * block, width), F32),
-                pltpu.VMEM((2, LANES, LANES), F32),
-                pltpu.VMEM((2, 2, group, block, width), F32),
-                pltpu.SemaphoreType.DMA((group + 2,)),
-            ],
-            input_output_aliases={aliased: 0, aliased + 1: 1},
+        last = g == groups - 1
+        args = [slow[g], slow_levels, levels, lhs, tiles, edge, middle, *total]
+        shapes = [(2, block, width), (2, 2, group, block, width)]
+        scratch = [pltpu.VMEM((2 * block, width), F32), pltpu.VMEM((2, LANES, LANES), F32)]
+        outs = shapes
+        if last:
+            args += [own_done, own_sum, *parts]
+            outs = [waves.shape, (STEPS, rows, width)]
+            scratch = [pltpu.VMEM(shape, F32) for shape in shapes] + scratch
+            scratch.append(pltpu.SemaphoreType.DMA((groups + group + 5,)))
+        result = pl.pallas_call(
+            functools.partial(second_kernel, g * group, g == 0, last),
+            out_shape=[jax.ShapeDtypeStruct(shape, F32) for shape in outs],
+            in_specs=[VMEM] * len(args),
+            out_specs=[ANY if last else VMEM] * len(outs),
+            scratch_shapes=scratch,
             compiler_params=pltpu.CompilerParams(vmem_limit_bytes=LIMIT),
             cost_estimate=pl.CostEstimate(flops=dots // groups, bytes_accessed=4 << 20, transcendentals=0),
             name=f"edge_rows_{g}",
-        )(slow[g], slow_levels, levels, lhs, tiles, edge, middle, *total, waves_out, image)
-    return waves_out, image
+        )(*args)
+        total = result[:1]
+        parts.append(result[1])
+    return tuple(result)
 
 
 def solution(mesh):

time: 21.6 us -> 19.4 us (0.90)
  waiting for transfers between devices: 3.97 us -> 1.36 us
  Pallas kernels: 11.1 us -> 9.82 us
  local copies, waits for them, and re-layouts: 1.71 us -> 2.93 us
  starting transfers between devices: 3.88 us -> 4.29 us
    ppermute x1, waiting for transfers between devices: 3.32 us -> 0.01 us  [on_device(): slow = [lax.ppermute(side(waves, slow_row, 0, group), axes, across)]]
    pallas_call x2 -> x3, Pallas kernels: 11.1 us -> 9.82 us  [the longest x1 5.79 us: on_device(): pl.pallas_call(first_kernel, out_shape=[jax.ShapeDtypeStruct((2, 2, freqs...]
    slice x0 -> x2, local copies, waits for them, and re-layouts: none -> 1.08 us  [side(): return cells[:, :, low:high].reshape(-1, block, width)]
    ppermute x1 -> x2, waiting for transfers between devices: 0.29 us -> 1.16 us  [the longest x1 1.16 us: on_device(): lax.ppermute(side(cells, slow_row, g * group, (g + 1) * group), axes, acr...]
    ppermute x1, starting transfers between devices: 1.2 us -> 1.86 us  [on_device(): slow = [lax.ppermute(side(waves, slow_row, 0, group), axes, across)]]
    unnamed x11, local copies, waits for them, and re-layouts: 0.3 us -> 0.69 us
    ppermute x1, starting transfers between devices: 1.5 us -> 1.2 us  [on_device(): lax.ppermute(lax.dynamic_slice_in_dim(marks, slow_row, block, axis=0), ax...]
    dynamic_slice x1, local copies, waits for them, and re-layouts: 1.37 us -> 1.11 us  [side(): cells = lax.dynamic_slice_in_dim(cells, start, block, axis=3)]
  transfers between devices with their start and end apart: 4 -> 5, of which waited for: 3 -> 2; matrix products, arithmetic and copies ran while one was open for 0% -> 6% of each run, Pallas kernels for 35% -> 39%
where the time goes in v1:
time: 19.4 us; the launch traced here: 19.2 us
  Pallas kernels  9.82 us (51%)
  starting transfers between devices  4.29 us (22%)
  local copies, waits for them, and re-layouts  2.93 us (15%)
  waiting for transfers between devices  1.36 us (7%)
  between operations  0.75 us (4%)
    pallas_call x1, Pallas kernels, on_device(): pl.pallas_call(first_kernel, out_shape=[jax.ShapeDtypeStruct((2, 2, freqs...  5.79 us
    pallas_call x2, Pallas kernels, on_device(): pl.pallas_call(functools.partial(second_kernel, g * group, g == 0, last),...  4.03 us
    ppermute x1, starting transfers between devices, on_device(): slow = [lax.ppermute(side(waves, slow_row, 0, group), axes, across)]  1.86 us
    ppermute x1, starting transfers between devices, on_device(): lax.ppermute(lax.dynamic_slice_in_dim(marks, slow_row, block, axis=0), ax...  1.2 us
    ppermute x1, waiting for transfers between devices, on_device(): lax.ppermute(side(cells, slow_row, g * group, (g + 1) * group), axes, acr...  1.16 us
    dynamic_slice x1, local copies, waits for them, and re-layouts, side(): cells = lax.dynamic_slice_in_dim(cells, start, block, axis=3)  1.11 us
    slice x2, local copies, waits for them, and re-layouts, side(): return cells[:, :, low:high].reshape(-1, block, width)  1.08 us
    unnamed x11, local copies, waits for them, and re-layouts  0.69 us
  transfers between devices with their start and end apart: 5, of which 2 were waited for; matrix products, arithmetic and copies ran while one was open for 6% of the time, Pallas kernels for 39%

profile of v1, /device:TPU:9, one launch (start us, length us, event | category | flops | bytes accessed | tf_op | source)
XLA Modules:
  0.0 19.2 jit_solution(11806401401475408177)
XLA Ops:
  0.6 0.0 copy-start
  0.7 1.1 %constant_dynamic-slice_fusion = f32[2,2,2,16,512]{4,3,2,1,0:T(8,128)S(1)} fusion(f32[2,2,4,32,512]{4,3,2,1,0:T(8,128)} %waves_ref.1, s32[]{:T(128)S(6)} %select_n.18), kind=kLoop, calls=%fused_computation.3 | loop fusion | bytes 524292 | tf_op jit(solution)/shard_map/slice | solution.py:406
  1.7 1.9 %collective-permute-start.4 = (f32[8,16,512]{2,1,0:T(8,128)S(1)}, f32[8,16,512]{2,1,0:T(8,128)S(1)}, u32[]{:S(2)}, u32[]{:S(2)}) collective-permute-start(f32[8,16,512]{2,1,0:T(8,128)S(1)} %bitcast.8), channel_id=1, source_target_pairs={{0,16},{1,2},{2,1},{3,4},{4,3},{5,6},{6,5},{7,8},{8,7},{9,10},{10,... | collective-permute-start | bytes 786440 | tf_op jit(solution)/shard_map/ppermute | solution.py:419
  3.6 0.0 copy-start.1
  3.6 1.1 %constant_dynamic-slice_fusion.4 = f32[2,2,4,16,512]{4,3,2,1,0:T(8,128)S(1)} fusion(f32[2,2,4,32,512]{4,3,2,1,0:T(8,128)} %waves_ref.1, s32[]{:T(128)S(6)} %select_n.17), kind=kLoop, calls=%fused_computation.7 | loop fusion | bytes 1048580 | tf_op jit(solution)/shard_map/dynamic_slice | solution.py:405
  4.7 0.1 collective-permute-start.2
  4.8 0.0 copy-done.1
  4.8 0.5 %collective-permute-start.3 = (s32[16,512]{1,0:T(8,128)S(1)}, s32[16,512]{1,0:T(8,128)S(1)}, u32[]{:S(2)}, u32[]{:S(2)}) collective-permute-start(s32[16,512]{1,0:T(8,128)S(1)} %get-tuple-element.22), channel_id=1, source_target_pairs={{0,1},{1,0},{2,3},{3,2},{4,5},{5,4},{6,7},{7,6},{8,9},{9,8},{10,11... | collective-permute-start | bytes 98312 | tf_op jit(solution)/shard_map/ppermute | solution.py:423
  5.4 1.2 %collective-permute-start.1 = (s32[16,512]{1,0:T(8,128)S(1)}, s32[16,512]{1,0:T(8,128)S(1)}, u32[]{:S(2)}, u32[]{:S(2)}) collective-permute-start(s32[16,512]{1,0:T(8,128)S(1)} %get-tuple-element.23), channel_id=1, source_target_pairs={{0,16},{1,2},{2,1},{3,4},{4,3},{5,6},{6,5},{7,8},{8,7},{9,10},{10,... | collective-permute-start | bytes 98312 | tf_op jit(solution)/shard_map/ppermute | solution.py:424
  6.6 0.0 copy-done
  6.6 0.0 copy-start.3
  6.6 0.6 %collective-permute-start = (f32[8,16,512]{2,1,0:T(8,128)S(1)}, f32[8,16,512]{2,1,0:T(8,128)S(1)}, u32[]{:S(2)}, u32[]{:S(2)}) collective-permute-start(f32[8,16,512]{2,1,0:T(8,128)S(1)} %bitcast.9), channel_id=1, source_target_pairs={{0,16},{1,2},{2,1},{3,4},{4,3},{5,6},{6,5},{7,8},{8,7},{9,10},{10,... | collective-permute-start | bytes 786440 | tf_op jit(solution)/shard_map/ppermute | solution.py:426
  7.2 0.0 copy-done.4
  7.3 0.0 copy-done.3
  7.3 0.0 copy-start.2
  7.3 0.0 collective-permute-done.3.halo_ref
  7.3 0.0 collective-permute-done.2.fast_ref
  7.4 0.6 %copy-done.2 = s32[4]{0:T(128)S(1)} copy-done((s32[4]{0:T(128)S(1)}, s32[4]{0:T(128)}, u32[]{:S(2)}) %copy-start.2) | copy-done | bytes 40
  8.0 5.8 %own_rows.1 = (f32[2,2,4,16,512]{4,3,2,1,0:T(8,128)S(1)}, f32[3,16,512]{2,1,0:T(8,128)S(1)}, bf16[4,2,2,2,16,512]{5,4,3,2,1,0:T(8,128)(2,1)S(1)}, bf16[4,2,2,2,1...) custom-call(s32[4]{0:T(128)S(1)} %copy-done.2, ...), custom_call_target="tpu_custom_call" | custom-call | flops 4026531840 | bytes 8388608 | tf_op jit(solution)/shard_map/own_rows/pallas_call | solution.py:432
  13.8 0.2 %collective-permute-done.1.halo_ref = s32[16,512]{1,0:T(8,128)S(1)} collective-permute-done((s32[16,512]{1,0:T(8,128)S(1)}, s32[16,512]{1,0:T(8,128)S(1)}, u32[]{:S(2)}, u32[]{:S(2)}) %collective-permute-start.1) | collective-permute-done | bytes 32800 | tf_op jit(solution)/shard_map/ppermute | solution.py:424
  14.0 0.0 collective-permute-done.4.slow_ref
  14.0 1.6 %edge_rows_0.1 = (f32[2,16,512]{2,1,0:T(8,128)S(1)}, f32[2,2,2,16,512]{4,3,2,1,0:T(8,128)S(1)}) custom-call(f32[8,16,512]{2,1,0:T(8,128)S(1)} %collective-permute-done.4.slow_ref, s32[16,512]{1,0:T(8,128)S(1)} %collective-permute-done.1.halo_ref, s32[32,512]{1,0:T(8,128)S(1)} %copy-done.1, bf16[2,4,160,256]{3,2,1,0:T(8,128)(2,1)S(1)} %get-tuple-element.14.lhs_ref, ...), custom_call_target="tpu_custom_call" | custom-call | flops 1006632960 | bytes 4194304 | tf_op jit(solution)/shard_map/edge_rows_0/pallas_call | solution.py:465
  15.6 1.2 %collective-permute-done.slow_ref = f32[8,16,512]{2,1,0:T(8,128)S(1)} collective-permute-done((f32[8,16,512]{2,1,0:T(8,128)S(1)}, f32[8,16,512]{2,1,0:T(8,128)S(1)}, u32[]{:S(2)}, u32[]{:S(2)}) %collective-permute-start) | collective-permute-done | bytes 262176 | tf_op jit(solution)/shard_map/ppermute | solution.py:426
  16.8 2.4 %edge_rows_1.1 = (f32[2,2,4,32,512]{4,3,2,1,0:T(8,128)}, f32[2,32,512]{2,1,0:T(8,128)}) custom-call(f32[8,16,512]{2,1,0:T(8,128)S(1)} %collective-permute-done.slow_ref, s32[16,512]{1,0:T(8,128)S(1)} %collective-permute-done.1.halo_ref, s32[32,512]{1,0:T(8,128)S(1)} %copy-done.1, bf16[2,4,160,256]{3,2,1,0:T(8,128)(2,1)S(1)} %get-tuple-element.14.lhs_ref, ...), custom_call_target="tpu_custom_call" | custom-call | flops 1006632960 | bytes 4194304 | tf_op jit(solution)/shard_map/edge_rows_1/pallas_call | solution.py:465
  (6 shorter events, 0.1 us)
Async XLA Ops:
  0.6 5.9 %copy-start = (f32[2,2,4,32,512]{4,3,2,1,0:T(8,128)S(1)}, f32[2,2,4,32,512]{4,3,2,1,0:T(8,128)}, u32[]{:S(2)}) copy-start(f32[2,2,4,32,512]{4,3,2,1,0:T(8,128)} %waves_ref.1) | copy-start | bytes 3145732
  1.7 12.2 %collective-permute-start.4 = (f32[8,16,512]{2,1,0:T(8,128)S(1)}, f32[8,16,512]{2,1,0:T(8,128)S(1)}, u32[]{:S(2)}, u32[]{:S(2)}) collective-permute-start(f32[8,16,512]{2,1,0:T(8,128)S(1)} %bitcast.8), channel_id=1, source_target_pairs={{0,16},{1,2},{2,1},{3,4},{4,3},{5,6},{6,5},{7,8},{8,7},{9,10},{10,... | collective-permute-start | bytes 786440 | tf_op jit(solution)/shard_map/ppermute | solution.py:419
  3.6 1.2 %copy-start.1 = (s32[32,512]{1,0:T(8,128)S(1)}, s32[32,512]{1,0:T(8,128)}, u32[]{:S(2)}) copy-start(s32[32,512]{1,0:T(8,128)} %lev_ref.5) | copy-start | bytes 196612
  4.7 2.6 %collective-permute-start.2 = (f32[16,16,512]{2,1,0:T(8,128)S(1)}, f32[16,16,512]{2,1,0:T(8,128)S(1)}, u32[]{:S(2)}, u32[]{:S(2)}) collective-permute-start(f32[16,16,512]{2,1,0:T(8,128)S(1)} %bitcast.7), channel_id=1, source_target_pairs={{0,1},{1,0},{2,3},{3,2},{4,5},{5,4},{6,7},{7,6},{8,9},{9,8},{10,11... | collective-permute-start | bytes 1572872 | tf_op jit(solution)/shard_map/ppermute | solution.py:421
  4.8 2.5 %collective-permute-start.3 = (s32[16,512]{1,0:T(8,128)S(1)}, s32[16,512]{1,0:T(8,128)S(1)}, u32[]{:S(2)}, u32[]{:S(2)}) collective-permute-start(s32[16,512]{1,0:T(8,128)S(1)} %get-tuple-element.22), channel_id=1, source_target_pairs={{0,1},{1,0},{2,3},{3,2},{4,5},{5,4},{6,7},{7,6},{8,9},{9,8},{10,11... | collective-permute-start | bytes 98312 | tf_op jit(solution)/shard_map/ppermute | solution.py:423
  5.4 8.6 %collective-permute-start.1 = (s32[16,512]{1,0:T(8,128)S(1)}, s32[16,512]{1,0:T(8,128)S(1)}, u32[]{:S(2)}, u32[]{:S(2)}) collective-permute-start(s32[16,512]{1,0:T(8,128)S(1)} %get-tuple-element.23), channel_id=1, source_target_pairs={{0,16},{1,2},{2,1},{3,4},{4,3},{5,6},{6,5},{7,8},{8,7},{9,10},{10,... | collective-permute-start | bytes 98312 | tf_op jit(solution)/shard_map/ppermute | solution.py:424
  6.6 0.7 %copy-start.4 = (f32[4,5]{1,0:T(4,128)S(1)}, f32[4,5]{1,0:T(4,128)}, u32[]{:S(2)}) copy-start(f32[4,5]{1,0:T(4,128)} %param.8) | copy-start | bytes 244
  6.6 0.7 %copy-start.3 = (f32[2,4,5,17]{3,1,2,0:T(4,128)S(1)}, f32[2,4,5,17]{3,1,2,0:T(4,128)}, u32[]{:S(2)}) copy-start(f32[2,4,5,17]{3,1,2,0:T(4,128)} %param.7) | copy-start | bytes 8164
  6.6 10.2 %collective-permute-start = (f32[8,16,512]{2,1,0:T(8,128)S(1)}, f32[8,16,512]{2,1,0:T(8,128)S(1)}, u32[]{:S(2)}, u32[]{:S(2)}) collective-permute-start(f32[8,16,512]{2,1,0:T(8,128)S(1)} %bitcast.9), channel_id=1, source_target_pairs={{0,16},{1,2},{2,1},{3,4},{4,3},{5,6},{6,5},{7,8},{8,7},{9,10},{10,... | collective-permute-start | bytes 786440 | tf_op jit(solution)/shard_map/ppermute | solution.py:426
  7.3 0.7 %copy-start.2 = (s32[4]{0:T(128)S(1)}, s32[4]{0:T(128)}, u32[]{:S(2)}) copy-start(s32[4]{0:T(128)} %order_ref.1) | copy-start | bytes 52

commit v2 on v1

--- a/solution.py
+++ b/solution.py
@@ -29,34 +29,23 @@
     return high, (cells - high.astype(F32)).astype(BF16)
 
 
-def build_filters(coef_ref, order_ref, pad_ref, lhs_ref, block):
-    freqs = lhs_ref.shape[1]
+def build_filters(coef_ref, row_of, pad_ref, lhs_ref, wanted, block):
     levels, taps = coef_ref.shape[2:]
     pad_ref[...] = jnp.zeros_like(pad_ref)
     pad_ref[:, :, :levels, :taps] = coef_ref[...]
     wide = 2 * block
-    lane = lax.broadcasted_iota(jnp.int32, (block, LANES), 1)
-    early = (lane % wide) < block
-
-    def body(f, carry):
-        row = order_ref[f]
+    for n, f in enumerate(wanted):
+        row = row_of(f)
         real, imag = pad_ref[0, row], pad_ref[1, row]
         tables = (real - pltpu.roll(imag, wide, 1), imag + pltpu.roll(real, wide, 1))
+        tables = [table + pltpu.roll(table, 2 * wide, 1) for table in tables]
         for level in range(levels):
             for part in range(2):
                 line = jnp.broadcast_to(tables[part][level : level + 1], (block, LANES))
-                band = pltpu.roll(line, 0, 1, stride=1, stride_axis=0)
-                swapped = jnp.where(early, pltpu.roll(band, LANES - block, 1), pltpu.roll(band, block, 1))
+                high, low = split(pltpu.roll(line, 0, 1, stride=1, stride_axis=0))
                 at = (level * 2 + part) * block
-                for v, cells in enumerate((band, swapped)):
-                    high, low = split(cells)
-                    high = high.astype(F32)
-                    lhs_ref[v, f, at : at + block, :LANES] = (high + pltpu.roll(high, 2 * wide, 1)).astype(BF16)
-                    lhs_ref[v, f, at : at + block, LANES:] = low
-        return carry
-
-    for f in range(freqs):
-        body(f, 0)
+                lhs_ref[n, at : at + block, :LANES] = high
+                lhs_ref[n, at : at + block, LANES:] = low
 
 
 def band_product(lhs, reals, imags):
@@ -171,6 +160,14 @@
                 ref[f, i, kind, part] = blocks[i][kind][part]
 
 
+def ordered(swap, first, second):
+    both = [
+        [[(jnp.where(swap, y, x), jnp.where(swap, x, y)) for x, y in zip(p, q)] for p, q in zip(a, b)]
+        for a, b in zip(first, second)
+    ]
+    return [[[[pair[n] for pair in kind] for kind in field] for field in both] for n in range(2)]
+
+
 def crossline(lhs, first, second, masks, block):
     wide = 2 * LANES
     width = first[0][0][0].shape[1]
@@ -235,20 +232,24 @@
 
 
 def first_kernel(
-    order_ref, cs_ref, coef_ref, waves_ref, lev_ref, fast_ref, halo_ref,
+    meta_ref, coef_ref, waves_ref, lev_ref, fast_ref, halo_ref,
     done_ref, acc_ref, edge_ref, mid_ref, lhs_ref, turn_ref,
     pad_ref, levw_ref, levt_ref,
 ):
-    freqs = lhs_ref.shape[1]
+    freqs = lhs_ref.shape[0]
     levels, taps = coef_ref.shape[2:]
     block = taps - 1
     half = block // 2
     c = lax.axis_index("strip") % 2
+
+    def row_of(f):
+        return meta_ref[2 * freqs * levels + f].astype(jnp.int32)
+
     for f in range(freqs):
         for part in range(2):
             for l in range(levels):
-                turn_ref[f, part, l] = jnp.full(turn_ref.shape[3:], cs_ref[part, order_ref[f], l], F32)
-    build_filters(coef_ref, order_ref, pad_ref, lhs_ref, block)
+                turn_ref[f, part, l] = jnp.full(turn_ref.shape[3:], meta_ref[(part * freqs + row_of(f)) * levels + l], F32)
+    build_filters(coef_ref, row_of, pad_ref, lhs_ref, range(freqs), block)
     slow_row = pl.multiple_of(block * c, block)
     fast_row = pl.multiple_of(block * (1 - c), block)
     lev_slow = lev_ref[pl.ds(slow_row, block)].astype(F32)
@@ -272,25 +273,25 @@
             get = lambda i, p: fast_ref[(i * 2 + p) * freqs + f]
         fields = raw_fields(get, cosine, sine)
         yield
-        fields = yield from inline(lhs_ref[0, f], fields, lambda: level_masks(levt_ref[slot], levels), block)
+        fields = yield from inline(lhs_ref[f], fields, lambda: level_masks(levt_ref[slot], levels), block)
         ready[f, slot] = split_fields(fields)
         if slot == 0:
             save(edge_ref, f, ready[f, slot])
 
     def next_chain(f, slot):
         first, second = ((0, 1), (1, 2))[slot]
-        fields = yield from crossline(lhs_ref[c, f], ready[f, first], ready[f, second], masks[3 + slot], block)
+        fields = yield from crossline(lhs_ref[f], *ordered(c == 1, ready[f, first], ready[f, second]), masks[3 + slot], block)
         acc_ref[slot] += image_of(fields)
         cosine, sine = turn_tables(turn_ref, f, masks[3 + slot])
         fields = [rotate(field, cosine, sine) for field in fields]
         yield
-        fields = yield from inline(lhs_ref[0, f], fields, lambda: level_masks(levt_ref[3 + slot], levels), block)
+        fields = yield from inline(lhs_ref[f], fields, lambda: level_masks(levt_ref[3 + slot], levels), block)
         ready[f, 3 + slot] = split_fields(fields)
         if slot == 0:
             save(mid_ref, f, ready[f, 3])
 
     def last_chain(f):
-        fields = yield from crossline(lhs_ref[c, f], ready[f, 3], ready[f, 4], masks[1], block)
+        fields = yield from crossline(lhs_ref[f], *ordered(c == 1, ready[f, 3], ready[f, 4]), masks[1], block)
         acc_ref[2] += image_of(fields)
         put_done(done_ref, f, fields)
 
@@ -311,7 +312,7 @@
     else:
         sum_ref, done_ref, levw_ref, levt_ref = refs
     levels = turn_ref.shape[2]
-    block = lhs_ref.shape[2] // (2 * levels)
+    block = lhs_ref.shape[1] // (2 * levels)
     group = done_ref.shape[2]
     half = block // 2
     rows = lev_ref.shape[0]
@@ -352,10 +353,10 @@
         get = lambda i, p: slow_ref[(i * 2 + p) * group + g]
         fields = raw_fields(get, cosine, sine)
         yield
-        fields = yield from inline(lhs_ref[0, f], fields, lambda: level_masks(levt_ref[0], levels), block)
+        fields = yield from inline(lhs_ref[f], fields, lambda: level_masks(levt_ref[0], levels), block)
         outer = split_fields(fields)
         yield
-        fields = yield from crossline(lhs_ref[1 - c, f], saved(edge_ref, f), outer, masks_edge, block)
+        fields = yield from crossline(lhs_ref[f], *ordered(c == 0, saved(edge_ref, f), outer), masks_edge, block)
         sum_ref[0] += image_of(fields)
         cosine, sine = [keep * t for t in turn_tables(turn_ref, f, masks_edge)]
         fields = [rotate(field, cosine, sine) for field in fields]
@@ -364,10 +365,10 @@
             own_row = pl.multiple_of(half * (1 - c), half)
             edge_row = pl.multiple_of((rows - half) * c, half)
             send(sum_ref.at[0, pl.ds(own_row, half)], img_ref.at[0, pl.ds(edge_row, half)])
-        fields = yield from inline(lhs_ref[0, f], fields, lambda: level_masks(levt_ref[1], levels), block)
+        fields = yield from inline(lhs_ref[f], fields, lambda: level_masks(levt_ref[1], levels), block)
         outer = split_fields(fields)
         yield
-        fields = yield from crossline(lhs_ref[1 - c, f], saved(mid_ref, f), outer, masks_near, block)
+        fields = yield from crossline(lhs_ref[f], *ordered(c == 0, saved(mid_ref, f), outer), masks_near, block)
         sum_ref[1] += image_of(fields)
         put_done(done_ref, g, fields)
         if last:
@@ -425,10 +426,10 @@
     for g in range(1, groups):
         slow.append(lax.ppermute(side(cells, slow_row, g * group, (g + 1) * group), axes, across))
 
-    turns = jnp.stack([jnp.cos(angles), jnp.sin(angles)])
-    lhs_shape = (2, freqs, 2 * level_count * block, 2 * LANES)
+    meta = jnp.concatenate([jnp.cos(angles).ravel(), jnp.sin(angles).ravel(), order.astype(F32)])
+    lhs_shape = (freqs, 2 * level_count * block, 2 * LANES)
     state = (freqs, 2, 2, 2, block, width)
-    dots = 16 * freqs * 2 * lhs_shape[2] * 12 * block * width
+    dots = 16 * freqs * 2 * lhs_shape[1] * 12 * block * width
     own_done, own_sum, edge, middle, lhs, tiles = pl.pallas_call(
         first_kernel,
         out_shape=[
@@ -439,7 +440,7 @@
             jax.ShapeDtypeStruct(lhs_shape, BF16),
             jax.ShapeDtypeStruct((freqs, 2, level_count, 8, LANES), F32),
         ],
-        in_specs=[SMEM, SMEM, VMEM, VMEM, VMEM, VMEM, VMEM],
+        in_specs=[SMEM, VMEM, VMEM, VMEM, VMEM, VMEM],
         out_specs=[VMEM] * 6,
         scratch_shapes=[
             pltpu.VMEM(coeffs.shape[:2] + (8, LANES), F32),
@@ -449,7 +450,7 @@
         compiler_params=pltpu.CompilerParams(vmem_limit_bytes=LIMIT),
         cost_estimate=pl.CostEstimate(flops=2 * dots, bytes_accessed=8 << 20, transcendentals=0),
         name="own_rows",
-    )(order, turns, coeffs, waves, levels, fast, fast_levels)
+    )(meta, coeffs, waves, levels, fast, fast_levels)
     total, parts = [], []
     for g in range(groups):
         last = g == groups - 1

time: 19.4 us -> 19.4 us (level)
  waiting for transfers between devices: 1.36 us -> 2.45 us
  Pallas kernels: 9.82 us -> 9.11 us
  local copies, waits for them, and re-layouts: 2.93 us -> 2.49 us
    ppermute x1, waiting for transfers between devices: 0.2 us -> 1.29 us  [on_device(): lax.ppermute(lax.dynamic_slice_in_dim(marks, slow_row, block, axis=0), ax...]
    pallas_call x1, Pallas kernels: 5.79 us -> 5.08 us  [on_device(): pl.pallas_call(first_kernel, out_shape=[jax.ShapeDtypeStruct((2, 2, freqs...]
    unnamed x11, local copies, waits for them, and re-layouts: 0.69 us -> 0.07 us
  transfers between devices with their start and end apart: 5 -> 5, of which waited for: 2 -> 2; matrix products, arithmetic and copies ran while one was open for 6% -> 7% of each run, Pallas kernels for 39% -> 35%
where the time goes in v2:
time: 19.4 us; the launch traced here: 19.2 us
  Pallas kernels  9.11 us (47%)
  starting transfers between devices  4.29 us (22%)
  local copies, waits for them, and re-layouts  2.49 us (13%)
  waiting for transfers between devices  2.45 us (13%)
  between operations  0.75 us (4%)
    pallas_call x1, Pallas kernels, on_device(): pl.pallas_call(first_kernel, out_shape=[jax.ShapeDtypeStruct((2, 2, freqs...  5.08 us
    pallas_call x2, Pallas kernels, on_device(): pl.pallas_call(functools.partial(second_kernel, g * group, g == 0, last),...  4.03 us
    ppermute x1, starting transfers between devices, on_device(): slow = [lax.ppermute(side(waves, slow_row, 0, group), axes, across)]  1.86 us
    ppermute x1, waiting for transfers between devices, on_device(): lax.ppermute(lax.dynamic_slice_in_dim(marks, slow_row, block, axis=0), ax...  1.29 us
    ppermute x1, starting transfers between devices, on_device(): lax.ppermute(lax.dynamic_slice_in_dim(marks, slow_row, block, axis=0), ax...  1.2 us
    ppermute x1, waiting for transfers between devices, on_device(): lax.ppermute(side(cells, slow_row, g * group, (g + 1) * group), axes, acr...  1.16 us
    dynamic_slice x1, local copies, waits for them, and re-layouts, side(): cells = lax.dynamic_slice_in_dim(cells, start, block, axis=3)  1.11 us
    slice x2, local copies, waits for them, and re-layouts, side(): return cells[:, :, low:high].reshape(-1, block, width)  1.08 us
  transfers between devices with their start and end apart: 5, of which 2 were waited for; matrix products, arithmetic and copies ran while one was open for 7% of the time, Pallas kernels for 35%

profile of v2, /device:TPU:9, one launch (start us, length us, event | category | flops | bytes accessed | tf_op | source)
XLA Modules:
  0.0 19.2 jit_solution(13419526308889213133)
XLA Ops:
  0.6 0.0 copy-start
  0.7 1.1 %constant_dynamic-slice_fusion = f32[2,2,2,16,512]{4,3,2,1,0:T(8,128)S(1)} fusion(f32[2,2,4,32,512]{4,3,2,1,0:T(8,128)} %waves_ref.1, s32[]{:T(128)S(6)} %select_n.18), kind=kLoop, calls=%fused_computation | loop fusion | bytes 524292 | tf_op jit(solution)/shard_map/slice | solution.py:407
  1.7 1.9 %collective-permute-start.4 = (f32[8,16,512]{2,1,0:T(8,128)S(1)}, f32[8,16,512]{2,1,0:T(8,128)S(1)}, u32[]{:S(2)}, u32[]{:S(2)}) collective-permute-start(f32[8,16,512]{2,1,0:T(8,128)S(1)} %bitcast.4), channel_id=1, source_target_pairs={{0,16},{1,2},{2,1},{3,4},{4,3},{5,6},{6,5},{7,8},{8,7},{9,10},{10,... | collective-permute-start | bytes 786440 | tf_op jit(solution)/shard_map/ppermute | solution.py:420
  3.6 1.1 %constant_dynamic-slice_fusion.4 = f32[2,2,4,16,512]{4,3,2,1,0:T(8,128)S(1)} fusion(f32[2,2,4,32,512]{4,3,2,1,0:T(8,128)} %waves_ref.1, s32[]{:T(128)S(6)} %select_n.17), kind=kLoop, calls=%fused_computation.4 | loop fusion | bytes 1048580 | tf_op jit(solution)/shard_map/dynamic_slice | solution.py:406
  4.7 0.1 collective-permute-start.2
  4.8 0.0 copy-done.1
  4.8 0.5 %collective-permute-start.3 = (s32[16,512]{1,0:T(8,128)S(1)}, s32[16,512]{1,0:T(8,128)S(1)}, u32[]{:S(2)}, u32[]{:S(2)}) collective-permute-start(s32[16,512]{1,0:T(8,128)S(1)} %get-tuple-element.22), channel_id=1, source_target_pairs={{0,1},{1,0},{2,3},{3,2},{4,5},{5,4},{6,7},{7,6},{8,9},{9,8},{10,11... | collective-permute-start | bytes 98312 | tf_op jit(solution)/shard_map/ppermute | solution.py:424
  5.4 1.2 %collective-permute-start.1 = (s32[16,512]{1,0:T(8,128)S(1)}, s32[16,512]{1,0:T(8,128)S(1)}, u32[]{:S(2)}, u32[]{:S(2)}) collective-permute-start(s32[16,512]{1,0:T(8,128)S(1)} %get-tuple-element.23), channel_id=1, source_target_pairs={{0,16},{1,2},{2,1},{3,4},{4,3},{5,6},{6,5},{7,8},{8,7},{9,10},{10,... | collective-permute-start | bytes 98312 | tf_op jit(solution)/shard_map/ppermute | solution.py:425
  6.6 0.0 copy-done
  6.6 0.0 copy-start.2
  6.6 0.6 %collective-permute-start = (f32[8,16,512]{2,1,0:T(8,128)S(1)}, f32[8,16,512]{2,1,0:T(8,128)S(1)}, u32[]{:S(2)}, u32[]{:S(2)}) collective-permute-start(f32[8,16,512]{2,1,0:T(8,128)S(1)} %bitcast.5), channel_id=1, source_target_pairs={{0,16},{1,2},{2,1},{3,4},{4,3},{5,6},{6,5},{7,8},{8,7},{9,10},{10,... | collective-permute-start | bytes 786440 | tf_op jit(solution)/shard_map/ppermute | solution.py:427
  7.2 0.0 copy-done.4
  7.2 0.0 copy-done.3
  7.3 0.1 reshape.21
  7.4 0.1 reshape.22
  7.5 0.1 pad_maximum_fusion.meta_ref
  7.6 0.0 collective-permute-done.3.halo_ref
  7.6 0.0 collective-permute-done.2.fast_ref
  7.6 5.1 %own_rows.1 = (f32[2,2,4,16,512]{4,3,2,1,0:T(8,128)S(1)}, f32[3,16,512]{2,1,0:T(8,128)S(1)}, bf16[4,2,2,2,16,512]{5,4,3,2,1,0:T(8,128)(2,1)S(1)}, bf16[4,2,2,2,1...) custom-call(f32[44]{0:T(128)S(1)} %pad_maximum_fusion.meta_ref, ...), custom_call_target="tpu_custom_call" | custom-call | flops 4026531840 | bytes 8388608 | tf_op jit(solution)/shard_map/own_rows/pallas_call | solution.py:433
  12.7 1.3 %collective-permute-done.1.halo_ref = s32[16,512]{1,0:T(8,128)S(1)} collective-permute-done((s32[16,512]{1,0:T(8,128)S(1)}, s32[16,512]{1,0:T(8,128)S(1)}, u32[]{:S(2)}, u32[]{:S(2)}) %collective-permute-start.1) | collective-permute-done | bytes 32800 | tf_op jit(solution)/shard_map/ppermute | solution.py:425
  14.0 0.0 collective-permute-done.4.slow_ref
  14.0 1.6 %edge_rows_0.1 = (f32[2,16,512]{2,1,0:T(8,128)S(1)}, f32[2,2,2,16,512]{4,3,2,1,0:T(8,128)S(1)}) custom-call(f32[8,16,512]{2,1,0:T(8,128)S(1)} %collective-permute-done.4.slow_ref, s32[16,512]{1,0:T(8,128)S(1)} %collective-permute-done.1.halo_ref, s32[32,512]{1,0:T(8,128)S(1)} %copy-done.1, bf16[4,160,256]{2,1,0:T(8,128)(2,1)S(1)} %get-tuple-element.14.lhs_ref, ...), custom_call_target="tpu_custom_call" | custom-call | flops 1006632960 | bytes 4194304 | tf_op jit(solution)/shard_map/edge_rows_0/pallas_call | solution.py:466
  15.6 1.2 %collective-permute-done.slow_ref = f32[8,16,512]{2,1,0:T(8,128)S(1)} collective-permute-done((f32[8,16,512]{2,1,0:T(8,128)S(1)}, f32[8,16,512]{2,1,0:T(8,128)S(1)}, u32[]{:S(2)}, u32[]{:S(2)}) %collective-permute-start) | collective-permute-done | bytes 262176 | tf_op jit(solution)/shard_map/ppermute | solution.py:427
  16.8 2.4 %edge_rows_1.1 = (f32[2,2,4,32,512]{4,3,2,1,0:T(8,128)}, f32[2,32,512]{2,1,0:T(8,128)}) custom-call(f32[8,16,512]{2,1,0:T(8,128)S(1)} %collective-permute-done.slow_ref, s32[16,512]{1,0:T(8,128)S(1)} %collective-permute-done.1.halo_ref, s32[32,512]{1,0:T(8,128)S(1)} %copy-done.1, bf16[4,160,256]{2,1,0:T(8,128)(2,1)S(1)} %get-tuple-element.14.lhs_ref, ...), custom_call_target="tpu_custom_call" | custom-call | flops 1006632960 | bytes 4194304 | tf_op jit(solution)/shard_map/edge_rows_1/pallas_call | solution.py:466
  (9 shorter events, 0.1 us)
Async XLA Ops:
  0.6 5.9 %copy-start = (f32[2,2,4,32,512]{4,3,2,1,0:T(8,128)S(1)}, f32[2,2,4,32,512]{4,3,2,1,0:T(8,128)}, u32[]{:S(2)}) copy-start(f32[2,2,4,32,512]{4,3,2,1,0:T(8,128)} %waves_ref.1) | copy-start | bytes 3145732
  1.7 12.2 %collective-permute-start.4 = (f32[8,16,512]{2,1,0:T(8,128)S(1)}, f32[8,16,512]{2,1,0:T(8,128)S(1)}, u32[]{:S(2)}, u32[]{:S(2)}) collective-permute-start(f32[8,16,512]{2,1,0:T(8,128)S(1)} %bitcast.4), channel_id=1, source_target_pairs={{0,16},{1,2},{2,1},{3,4},{4,3},{5,6},{6,5},{7,8},{8,7},{9,10},{10,... | collective-permute-start | bytes 786440 | tf_op jit(solution)/shard_map/ppermute | solution.py:420
  3.6 1.2 %copy-start.1 = (s32[32,512]{1,0:T(8,128)S(1)}, s32[32,512]{1,0:T(8,128)}, u32[]{:S(2)}) copy-start(s32[32,512]{1,0:T(8,128)} %lev_ref.5) | copy-start | bytes 196612
  4.7 2.9 %collective-permute-start.2 = (f32[16,16,512]{2,1,0:T(8,128)S(1)}, f32[16,16,512]{2,1,0:T(8,128)S(1)}, u32[]{:S(2)}, u32[]{:S(2)}) collective-permute-start(f32[16,16,512]{2,1,0:T(8,128)S(1)} %bitcast.3), channel_id=1, source_target_pairs={{0,1},{1,0},{2,3},{3,2},{4,5},{5,4},{6,7},{7,6},{8,9},{9,8},{10,11... | collective-permute-start | bytes 1572872 | tf_op jit(solution)/shard_map/ppermute | solution.py:422
  4.8 2.8 %collective-permute-start.3 = (s32[16,512]{1,0:T(8,128)S(1)}, s32[16,512]{1,0:T(8,128)S(1)}, u32[]{:S(2)}, u32[]{:S(2)}) collective-permute-start(s32[16,512]{1,0:T(8,128)S(1)} %get-tuple-element.22), channel_id=1, source_target_pairs={{0,1},{1,0},{2,3},{3,2},{4,5},{5,4},{6,7},{7,6},{8,9},{9,8},{10,11... | collective-permute-start | bytes 98312 | tf_op jit(solution)/shard_map/ppermute | solution.py:424
  5.4 8.6 %collective-permute-start.1 = (s32[16,512]{1,0:T(8,128)S(1)}, s32[16,512]{1,0:T(8,128)S(1)}, u32[]{:S(2)}, u32[]{:S(2)}) collective-permute-start(s32[16,512]{1,0:T(8,128)S(1)} %get-tuple-element.23), channel_id=1, source_target_pairs={{0,16},{1,2},{2,1},{3,4},{4,3},{5,6},{6,5},{7,8},{8,7},{9,10},{10,... | collective-permute-start | bytes 98312 | tf_op jit(solution)/shard_map/ppermute | solution.py:425
  6.6 0.7 %copy-start.4 = (s32[4]{0:T(128)S(1)}, s32[4]{0:T(128)}, u32[]{:S(2)}) copy-start(s32[4]{0:T(128)} %param.9) | copy-start | bytes 52
  6.6 0.7 %copy-start.3 = (f32[4,5]{1,0:T(4,128)S(1)}, f32[4,5]{1,0:T(4,128)}, u32[]{:S(2)}) copy-start(f32[4,5]{1,0:T(4,128)} %param.8) | copy-start | bytes 244
  6.6 1.0 %copy-start.2 = (f32[2,4,5,17]{3,1,2,0:T(4,128)S(1)}, f32[2,4,5,17]{3,1,2,0:T(4,128)}, u32[]{:S(2)}) copy-start(f32[2,4,5,17]{3,1,2,0:T(4,128)} %param.7) | copy-start | bytes 8164
  6.6 10.2 %collective-permute-start = (f32[8,16,512]{2,1,0:T(8,128)S(1)}, f32[8,16,512]{2,1,0:T(8,128)S(1)}, u32[]{:S(2)}, u32[]{:S(2)}) collective-permute-start(f32[8,16,512]{2,1,0:T(8,128)S(1)} %bitcast.5), channel_id=1, source_target_pairs={{0,16},{1,2},{2,1},{3,4},{4,3},{5,6},{6,5},{7,8},{8,7},{9,10},{10,... | collective-permute-start | bytes 786440 | tf_op jit(solution)/shard_map/ppermute | solution.py:427

commit v3 on v2

--- a/solution.py
+++ b/solution.py
@@ -30,9 +30,8 @@
 
 
 def build_filters(coef_ref, row_of, pad_ref, lhs_ref, wanted, block):
-    levels, taps = coef_ref.shape[2:]
-    pad_ref[...] = jnp.zeros_like(pad_ref)
-    pad_ref[:, :, :levels, :taps] = coef_ref[...]
+    levels = lhs_ref.shape[1] // (2 * block)
+    pad_ref = coef_ref
     wide = 2 * block
     for n, f in enumerate(wanted):
         row = row_of(f)
@@ -231,25 +230,64 @@
     return ref[block // 2 : block // 2 + block]
 
 
+def early_kernel(
+    meta_ref, coef_ref, raw_ref, lev_ref,
+    sent_ref, edge_ref, lhs_ref, turn_ref,
+    pad_ref, levt_ref,
+):
+    freqs = turn_ref.shape[0]
+    block = raw_ref.shape[1]
+    levels = lhs_ref.shape[1] // (2 * block)
+    later = edge_ref.shape[0]
+    c = lax.axis_index("strip") % 2
+
+    def row_of(f):
+        return meta_ref[2 * freqs * levels + f].astype(jnp.int32)
+
+    for f in range(freqs):
+        for part in range(2):
+            for l in range(levels):
+                turn_ref[f, part, l] = jnp.full(
+                    turn_ref.shape[3:], meta_ref[(part * freqs + row_of(f)) * levels + l], F32
+                )
+    build_filters(coef_ref, row_of, pad_ref, lhs_ref, range(freqs - later, freqs), block)
+    slow_row = pl.multiple_of(block * c, block)
+    lev = lev_ref[pl.ds(slow_row, block)].astype(F32)
+    levt_ref[...] = to_columns([lev, lev], block)
+    masks = level_masks(lev, levels)
+
+    def chain(n):
+        f = freqs - later + n
+        cosine, sine = turn_tables(turn_ref, f, masks)
+        fields = raw_fields(lambda i, p: raw_ref[(i * 2 + p) * later + n], cosine, sine)
+        yield
+        fields = yield from inline(lhs_ref[n], fields, lambda: level_masks(levt_ref[...], levels), block)
+        for i in range(2):
+            for p in range(2):
+                sent_ref[(i * 2 + p) * later + n] = fields[i][p]
+        save(edge_ref, n, split_fields(fields))
+
+    interleave([chain(n) for n in range(later)], SKEW1)
+
+
 def first_kernel(
-    meta_ref, coef_ref, waves_ref, lev_ref, fast_ref, halo_ref,
-    done_ref, acc_ref, edge_ref, mid_ref, lhs_ref, turn_ref,
+    meta_ref, coef_ref, waves_ref, lev_ref, fast_ref, halo_ref, early_lhs_ref, turn_ref, later_ref,
+    done_ref, acc_ref, edge_ref, mid_ref, lhs_ref,
     pad_ref, levw_ref, levt_ref,
 ):
     freqs = lhs_ref.shape[0]
-    levels, taps = coef_ref.shape[2:]
-    block = taps - 1
+    levels = turn_ref.shape[2]
+    block = lhs_ref.shape[1] // (2 * levels)
+    group = edge_ref.shape[0]
     half = block // 2
     c = lax.axis_index("strip") % 2
 
     def row_of(f):
         return meta_ref[2 * freqs * levels + f].astype(jnp.int32)
 
-    for f in range(freqs):
-        for part in range(2):
-            for l in range(levels):
-                turn_ref[f, part, l] = jnp.full(turn_ref.shape[3:], meta_ref[(part * freqs + row_of(f)) * levels + l], F32)
-    build_filters(coef_ref, row_of, pad_ref, lhs_ref, range(freqs), block)
+    build_filters(coef_ref, row_of, pad_ref, lhs_ref, range(group), block)
+    for f in range(group, freqs):
+        lhs_ref[f] = early_lhs_ref[f - group]
     slow_row = pl.multiple_of(block * c, block)
     fast_row = pl.multiple_of(block * (1 - c), block)
     lev_slow = lev_ref[pl.ds(slow_row, block)].astype(F32)
@@ -278,6 +316,9 @@
         if slot == 0:
             save(edge_ref, f, ready[f, slot])
 
+    for f in range(group, freqs):
+        ready[f, 0] = saved(later_ref, f - group)
+
     def next_chain(f, slot):
         first, second = ((0, 1), (1, 2))[slot]
         fields = yield from crossline(lhs_ref[f], *ordered(c == 1, ready[f, first], ready[f, second]), masks[3 + slot], block)
@@ -295,7 +336,7 @@
         acc_ref[2] += image_of(fields)
         put_done(done_ref, f, fields)
 
-    interleave([start_chain(f, slot) for f in range(freqs) for slot in range(3)], SKEW1)
+    interleave([start_chain(f, slot) for f in range(freqs) for slot in range(f >= group, 3)], SKEW1)
     interleave([next_chain(f, slot) for f in range(freqs) for slot in range(2)], SKEW1)
     interleave([last_chain(f) for f in range(freqs)], SKEW1)
 
@@ -349,14 +390,18 @@
 
     def chain(g):
         f = offset + g
-        cosine, sine = [inside * t for t in turn_tables(turn_ref, f, masks_halo)]
         get = lambda i, p: slow_ref[(i * 2 + p) * group + g]
-        fields = raw_fields(get, cosine, sine)
-        yield
-        fields = yield from inline(lhs_ref[f], fields, lambda: level_masks(levt_ref[0], levels), block)
+        if first:
+            cosine, sine = [inside * t for t in turn_tables(turn_ref, f, masks_halo)]
+            fields = raw_fields(get, cosine, sine)
+            yield
+            masks = lambda: level_masks(levt_ref[0], levels)
+            fields = yield from inline(lhs_ref[f], fields, masks, block)
+        else:
+            fields = [[inside * get(i, p) for p in range(2)] for i in range(2)]
         outer = split_fields(fields)
         yield
-        fields = yield from crossline(lhs_ref[f], *ordered(c == 0, saved(edge_ref, f), outer), masks_edge, block)
+        fields = yield from crossline(lhs_ref[f], *ordered(c == 0, saved(edge_ref, g), outer), masks_edge, block)
         sum_ref[0] += image_of(fields)
         cosine, sine = [keep * t for t in turn_tables(turn_ref, f, masks_edge)]
         fields = [rotate(field, cosine, sine) for field in fields]
@@ -388,7 +433,6 @@
 SKEW = 3
 SKEW1 = 2
 LAG = 1
-GROUPS = 2
 
 
 def on_device(waves, levels, coeffs, angles, order):
@@ -399,7 +443,7 @@
     count = lax.axis_size("strip")
     index = lax.axis_index("strip")
     c = index % 2
-    groups = GROUPS if freqs % GROUPS == 0 else 1
+    groups = 2
     group = freqs // groups
 
     def side(cells, start, low=0, high=freqs):
@@ -417,44 +461,56 @@
     axes = ("shot", "strip")
 
     slow_row, fast_row = c * (rows - block), (1 - c) * (rows - block)
-    slow = [lax.ppermute(side(waves, slow_row, 0, group), axes, across)]
+    meta = jnp.concatenate([jnp.cos(angles).ravel(), jnp.sin(angles).ravel(), order.astype(F32)])
+    lhs_shape = (freqs, 2 * level_count * block, 2 * LANES)
+    state = (2, 2, 2, block, width)
+    later = freqs - group
+    dots = 16 * freqs * 2 * lhs_shape[1] * 12 * block * width
+    taps_in = jnp.pad(coeffs, ((0, 0), (0, 0), (0, 8 - level_count), (0, LANES - taps)))
+    far = side(waves, slow_row, 0, group)
+    slow = [lax.ppermute(far, axes, across)]
     near = side(waves, fast_row)
     fast = lax.ppermute(near, axes, within)
     cells, marks, _ = lax.optimization_barrier((waves, levels, near))
+    sent, later_edge, early_lhs, tiles = pl.pallas_call(
+        early_kernel,
+        out_shape=[
+            jax.ShapeDtypeStruct((4 * later, block, width), F32),
+            jax.ShapeDtypeStruct((later,) + state, BF16),
+            jax.ShapeDtypeStruct((later,) + lhs_shape[1:], BF16),
+            jax.ShapeDtypeStruct((freqs, 2, level_count, 8, LANES), F32),
+        ],
+        in_specs=[SMEM, VMEM, VMEM, VMEM],
+        out_specs=[VMEM] * 4,
+        scratch_shapes=[pltpu.VMEM(coeffs.shape[:2] + (8, LANES), F32), pltpu.VMEM((LANES, LANES), F32)],
+        compiler_params=pltpu.CompilerParams(vmem_limit_bytes=LIMIT),
+        cost_estimate=pl.CostEstimate(flops=dots // 8, bytes_accessed=2 << 20, transcendentals=0),
+        name="early_rows",
+    )(meta, taps_in, side(cells, slow_row, group, freqs), marks)
     fast_levels = lax.ppermute(lax.dynamic_slice_in_dim(marks, fast_row, block, axis=0), axes, within)
     slow_levels = lax.ppermute(lax.dynamic_slice_in_dim(marks, slow_row, block, axis=0), axes, across)
-    for g in range(1, groups):
-        slow.append(lax.ppermute(side(cells, slow_row, g * group, (g + 1) * group), axes, across))
-
-    meta = jnp.concatenate([jnp.cos(angles).ravel(), jnp.sin(angles).ravel(), order.astype(F32)])
-    lhs_shape = (freqs, 2 * level_count * block, 2 * LANES)
-    state = (freqs, 2, 2, 2, block, width)
-    dots = 16 * freqs * 2 * lhs_shape[1] * 12 * block * width
-    own_done, own_sum, edge, middle, lhs, tiles = pl.pallas_call(
+    slow.append(lax.ppermute(sent, axes, across))
+    own_done, own_sum, edge, middle, lhs = pl.pallas_call(
         first_kernel,
         out_shape=[
             jax.ShapeDtypeStruct((2, 2, freqs, block, width), F32),
             jax.ShapeDtypeStruct((3, block, width), F32),
-            jax.ShapeDtypeStruct(state, BF16),
-            jax.ShapeDtypeStruct(state, BF16),
+            jax.ShapeDtypeStruct((group,) + state, BF16),
+            jax.ShapeDtypeStruct((freqs,) + state, BF16),
             jax.ShapeDtypeStruct(lhs_shape, BF16),
-            jax.ShapeDtypeStruct((freqs, 2, level_count, 8, LANES), F32),
         ],
-        in_specs=[SMEM, VMEM, VMEM, VMEM, VMEM, VMEM],
-        out_specs=[VMEM] * 6,
-        scratch_shapes=[
-            pltpu.VMEM(coeffs.shape[:2] + (8, LANES), F32),
-            pltpu.VMEM((2 * block, width), F32),
-            pltpu.VMEM((5, LANES, LANES), F32),
-        ],
+        in_specs=[SMEM] + [VMEM] * 8,
+        out_specs=[VMEM] * 5,
+        scratch_shapes=[pltpu.VMEM(coeffs.shape[:2] + (8, LANES), F32), pltpu.VMEM((2 * block, width), F32), pltpu.VMEM((5, LANES, LANES), F32)],
         compiler_params=pltpu.CompilerParams(vmem_limit_bytes=LIMIT),
         cost_estimate=pl.CostEstimate(flops=2 * dots, bytes_accessed=8 << 20, transcendentals=0),
         name="own_rows",
-    )(meta, coeffs, waves, levels, fast, fast_levels)
+    )(meta, taps_in, cells, marks, fast, fast_levels, early_lhs, tiles, later_edge)
+    edges = [edge, later_edge]
     total, parts = [], []
     for g in range(groups):
         last = g == groups - 1
-        args = [slow[g], slow_levels, levels, lhs, tiles, edge, middle, *total]
+        args = [slow[g], slow_levels, levels, lhs, tiles, edges[g], middle, *total]
         shapes = [(2, block, width), (2, 2, group, block, width)]
         scratch = [pltpu.VMEM((2 * block, width), F32), pltpu.VMEM((2, LANES, LANES), F32)]
         outs = shapes

time: 19.4 us -> 19.6 us (1.010)
  waiting for transfers between devices: 2.45 us -> 1.65 us
  local copies, waits for them, and re-layouts: 2.49 us -> 3.08 us
  Pallas kernels: 9.11 us -> 9.45 us
    ppermute x1, waiting for transfers between devices: 1.29 us -> 0.01 us  [on_device(): lax.ppermute(lax.dynamic_slice_in_dim(marks, slow_row, block, axis=0), ax...]
    pallas_call x0 -> x1, Pallas kernels: none -> 1.25 us  [on_device(): pl.pallas_call(early_kernel, out_shape=[jax.ShapeDtypeStruct((4 * later,...]
    unnamed x11, local copies, waits for them, and re-layouts: 0.07 us -> 0.65 us
    pallas_call x2, Pallas kernels: 4.03 us -> 3.53 us  [on_device(): pl.pallas_call(functools.partial(second_kernel, g * group, g == 0, last),...]
    ppermute x2, waiting for transfers between devices: 1.16 us -> 1.64 us  [the longest x1 1.64 us: on_device(): slow.append(lax.ppermute(sent, axes, across))]
    pallas_call x1, Pallas kernels: 5.08 us -> 4.67 us  [on_device(): pl.pallas_call(first_kernel, out_shape=[jax.ShapeDtypeStruct((2, 2, freqs...]
  transfers between devices with their start and end apart: 5 -> 5, of which waited for: 2 -> 1; matrix products, arithmetic and copies ran while one was open for 7% -> 7% of each run, Pallas kernels for 35% -> 39%
where the time goes in v3:
time: 19.6 us; the launch traced here: 19.4 us
  Pallas kernels  9.45 us (48%)
  starting transfers between devices  4.35 us (22%)
  local copies, waits for them, and re-layouts  3.08 us (16%)
  waiting for transfers between devices  1.65 us (8%)
  between operations  0.75 us (4%)
    pallas_call x1, Pallas kernels, on_device(): pl.pallas_call(first_kernel, out_shape=[jax.ShapeDtypeStruct((2, 2, freqs...  4.67 us
    pallas_call x2, Pallas kernels, on_device(): pl.pallas_call(functools.partial(second_kernel, g * group, g == 0, last),...  3.53 us
    ppermute x1, starting transfers between devices, on_device(): slow = [lax.ppermute(far, axes, across)]  1.86 us
    ppermute x1, waiting for transfers between devices, on_device(): slow.append(lax.ppermute(sent, axes, across))  1.64 us
    pallas_call x1, Pallas kernels, on_device(): pl.pallas_call(early_kernel, out_shape=[jax.ShapeDtypeStruct((4 * later,...  1.25 us
    ppermute x1, starting transfers between devices, on_device(): lax.ppermute(lax.dynamic_slice_in_dim(marks, slow_row, block, axis=0), ax...  1.21 us
    dynamic_slice x1, local copies, waits for them, and re-layouts, side(): cells = lax.dynamic_slice_in_dim(cells, start, block, axis=3)  1.11 us
    slice x2, local copies, waits for them, and re-layouts, side(): return cells[:, :, low:high].reshape(-1, block, width)  1.09 us
  transfers between devices with their start and end apart: 5, of which 1 were waited for; matrix products, arithmetic and copies ran while one was open for 7% of the time, Pallas kernels for 39%

profile of v3, /device:TPU:9, one launch (start us, length us, event | category | flops | bytes accessed | tf_op | source)
XLA Modules:
  0.0 19.4 jit_solution(15210915851416602250)
XLA Ops:
  0.6 0.0 copy-start
  0.7 1.1 %constant_dynamic-slice_fusion = f32[2,2,2,16,512]{4,3,2,1,0:T(8,128)S(1)} fusion(f32[2,2,4,32,512]{4,3,2,1,0:T(8,128)} %waves_ref, s32[]{:T(128)S(6)} %select_n.18), kind=kLoop, calls=%fused_computation | loop fusion | bytes 524292 | tf_op jit(solution)/shard_map/slice | solution.py:451
  1.7 1.9 %collective-permute-start.4 = (f32[8,16,512]{2,1,0:T(8,128)S(1)}, f32[8,16,512]{2,1,0:T(8,128)S(1)}, u32[]{:S(2)}, u32[]{:S(2)}) collective-permute-start(f32[8,16,512]{2,1,0:T(8,128)S(1)} %bitcast.5), channel_id=1, source_target_pairs={{0,16},{1,2},{2,1},{3,4},{4,3},{5,6},{6,5},{7,8},{8,7},{9,10},{10,... | collective-permute-start | bytes 786440 | tf_op jit(solution)/shard_map/ppermute | solution.py:471
  3.6 1.1 %constant_dynamic-slice_fusion.4 = f32[2,2,4,16,512]{4,3,2,1,0:T(8,128)S(1)} fusion(f32[2,2,4,32,512]{4,3,2,1,0:T(8,128)} %waves_ref, s32[]{:T(128)S(6)} %select_n.17), kind=kLoop, calls=%fused_computation.4 | loop fusion | bytes 1048580 | tf_op jit(solution)/shard_map/dynamic_slice | solution.py:450
  4.7 0.1 collective-permute-start.2
  4.8 0.0 copy-done.1
  4.8 0.0 copy-start.3
  4.8 0.5 %collective-permute-start.3 = (s32[16,512]{1,0:T(8,128)S(1)}, s32[16,512]{1,0:T(8,128)S(1)}, u32[]{:S(2)}, u32[]{:S(2)}) collective-permute-start(s32[16,512]{1,0:T(8,128)S(1)} %get-tuple-element.28), channel_id=1, source_target_pairs={{0,1},{1,0},{2,3},{3,2},{4,5},{5,4},{6,7},{7,6},{8,9},{9,8},{10,11... | collective-permute-start | bytes 98312 | tf_op jit(solution)/shard_map/ppermute | solution.py:490
  5.4 1.2 %collective-permute-start.1 = (s32[16,512]{1,0:T(8,128)S(1)}, s32[16,512]{1,0:T(8,128)S(1)}, u32[]{:S(2)}, u32[]{:S(2)}) collective-permute-start(s32[16,512]{1,0:T(8,128)S(1)} %get-tuple-element.29), channel_id=1, source_target_pairs={{0,16},{1,2},{2,1},{3,4},{4,3},{5,6},{6,5},{7,8},{8,7},{9,10},{10,... | collective-permute-start | bytes 98312 | tf_op jit(solution)/shard_map/ppermute | solution.py:491
  6.6 0.0 copy-done.4
  6.6 0.1 reshape.19
  6.7 0.1 reshape.20
  6.8 0.1 pad_maximum_fusion.meta_ref
  6.9 0.6 %copy-done.2 = f32[2,4,5,17]{3,1,2,0:T(4,128)S(1)} copy-done((f32[2,4,5,17]{3,1,2,0:T(4,128)S(1)}, f32[2,4,5,17]{3,1,2,0:T(4,128)}, u32[]{:S(2)}) %copy-start.2) | copy-done | bytes 2744
  7.5 1.3 %early_rows.1 = (f32[8,16,512]{2,1,0:T(8,128)S(1)}, bf16[2,2,2,2,16,512]{5,4,3,2,1,0:T(8,128)(2,1)S(1)}, bf16[2,160,256]{2,1,0:T(8,128)(2,1)S(1)}, f32[4,2,5,8,128]{4,3,2,1,0:T(8,128)S(1)}) custom-call(f32[44]{0:T(128)S(1)} %pad_maximum_fusion.meta_ref, f32[2,4,8,128]{3,2,1,0:T(8,128)S(1)} %pad.4.coef_ref, f32[8,16,512]{2,1,0:T(8,128)S(1)} %bitcast.3, ...), custom_call_target="tpu_custom_call" | custom-call | flops 251658240 | bytes 2097152 | tf_op jit(solution)/shard_map/early_rows/pallas_call | solution.py:475
  8.8 0.7 %collective-permute-start = (f32[8,16,512]{2,1,0:T(8,128)S(1)}, f32[8,16,512]{2,1,0:T(8,128)S(1)}, u32[]{:S(2)}, u32[]{:S(2)}) collective-permute-start(f32[8,16,512]{2,1,0:T(8,128)S(1)} %get-tuple-element.17), channel_id=1, source_target_pairs={{0,16},{1,2},{2,1},{3,4},{4,3},{5,6},{6,5},{7,8},{8,7},{9,10},{10,... | collective-permute-start | bytes 786440 | tf_op jit(solution)/shard_map/ppermute | solution.py:492
  9.5 0.0 collective-permute-done.3.halo_ref
  9.5 0.0 collective-permute-done.2.fast_ref
  9.5 4.7 %own_rows.1 = (f32[2,2,4,16,512]{4,3,2,1,0:T(8,128)S(1)}, f32[3,16,512]{2,1,0:T(8,128)S(1)}, bf16[2,2,2,2,16,512]{5,4,3,2,1,0:T(8,128)(2,1)S(1)}, bf16[4,2,2,2,1...) custom-call(f32[44]{0:T(128)S(1)} %pad_maximum_fusion.meta_ref, f32[2,4,8,128]{3,2,1,0:T(8,128)S(1)} %pad.4.coef_ref, ...), custom_call_target="tpu_custom_call" | custom-call | flops 4026531840 | bytes 8388608 | tf_op jit(solution)/shard_map/own_rows/pallas_call | solution.py:493
  14.2 0.0 collective-permute-done.1.halo_ref
  14.2 0.0 collective-permute-done.4.slow_ref
  14.2 1.7 %edge_rows_0.1 = (f32[2,16,512]{2,1,0:T(8,128)S(1)}, f32[2,2,2,16,512]{4,3,2,1,0:T(8,128)S(1)}) custom-call(f32[8,16,512]{2,1,0:T(8,128)S(1)} %collective-permute-done.4.slow_ref, s32[16,512]{1,0:T(8,128)S(1)} %collective-permute-done.1.halo_ref, s32[32,512]{1,0:T(8,128)S(1)} %copy-done.1, bf16[4,160,256]{2,1,0:T(8,128)(2,1)S(1)} %get-tuple-element.21.lhs_ref, ...), custom_call_target="tpu_custom_call" | custom-call | flops 1006632960 | bytes 4194304 | tf_op jit(solution)/shard_map/edge_rows_0/pallas_call | solution.py:522
  15.8 1.6 %collective-permute-done.slow_ref = f32[8,16,512]{2,1,0:T(8,128)S(1)} collective-permute-done((f32[8,16,512]{2,1,0:T(8,128)S(1)}, f32[8,16,512]{2,1,0:T(8,128)S(1)}, u32[]{:S(2)}, u32[]{:S(2)}) %collective-permute-start) | collective-permute-done | bytes 262176 | tf_op jit(solution)/shard_map/ppermute | solution.py:492
  17.5 1.9 %edge_rows_1.1 = (f32[2,2,4,32,512]{4,3,2,1,0:T(8,128)}, f32[2,32,512]{2,1,0:T(8,128)}) custom-call(f32[8,16,512]{2,1,0:T(8,128)S(1)} %collective-permute-done.slow_ref, s32[16,512]{1,0:T(8,128)S(1)} %collective-permute-done.1.halo_ref, s32[32,512]{1,0:T(8,128)S(1)} %copy-done.1, bf16[4,160,256]{2,1,0:T(8,128)(2,1)S(1)} %get-tuple-element.21.lhs_ref, ...), custom_call_target="tpu_custom_call" | custom-call | flops 1006632960 | bytes 4194304 | tf_op jit(solution)/shard_map/edge_rows_1/pallas_call | solution.py:522
  (11 shorter events, 0.1 us)
Async XLA Ops:
  0.6 6.2 %copy-start = (f32[2,2,4,32,512]{4,3,2,1,0:T(8,128)S(1)}, f32[2,2,4,32,512]{4,3,2,1,0:T(8,128)}, u32[]{:S(2)}) copy-start(f32[2,2,4,32,512]{4,3,2,1,0:T(8,128)} %waves_ref) | copy-start | bytes 3145732
  1.7 12.4 %collective-permute-start.4 = (f32[8,16,512]{2,1,0:T(8,128)S(1)}, f32[8,16,512]{2,1,0:T(8,128)S(1)}, u32[]{:S(2)}, u32[]{:S(2)}) collective-permute-start(f32[8,16,512]{2,1,0:T(8,128)S(1)} %bitcast.5), channel_id=1, source_target_pairs={{0,16},{1,2},{2,1},{3,4},{4,3},{5,6},{6,5},{7,8},{8,7},{9,10},{10,... | collective-permute-start | bytes 786440 | tf_op jit(solution)/shard_map/ppermute | solution.py:471
  3.6 1.2 %copy-start.1 = (s32[32,512]{1,0:T(8,128)S(1)}, s32[32,512]{1,0:T(8,128)}, u32[]{:S(2)}) copy-start(s32[32,512]{1,0:T(8,128)} %lev_ref.5) | copy-start | bytes 196612
  4.7 4.8 %collective-permute-start.2 = (f32[16,16,512]{2,1,0:T(8,128)S(1)}, f32[16,16,512]{2,1,0:T(8,128)S(1)}, u32[]{:S(2)}, u32[]{:S(2)}) collective-permute-start(f32[16,16,512]{2,1,0:T(8,128)S(1)} %bitcast.4), channel_id=1, source_target_pairs={{0,1},{1,0},{2,3},{3,2},{4,5},{5,4},{6,7},{7,6},{8,9},{9,8},{10,11... | collective-permute-start | bytes 1572872 | tf_op jit(solution)/shard_map/ppermute | solution.py:473
  4.8 1.8 %copy-start.3 = (f32[4,5]{1,0:T(4,128)S(1)}, f32[4,5]{1,0:T(4,128)}, u32[]{:S(2)}) copy-start(f32[4,5]{1,0:T(4,128)} %param.8) | copy-start | bytes 244
  4.8 4.6 %collective-permute-start.3 = (s32[16,512]{1,0:T(8,128)S(1)}, s32[16,512]{1,0:T(8,128)S(1)}, u32[]{:S(2)}, u32[]{:S(2)}) collective-permute-start(s32[16,512]{1,0:T(8,128)S(1)} %get-tuple-element.28), channel_id=1, source_target_pairs={{0,1},{1,0},{2,3},{3,2},{4,5},{5,4},{6,7},{7,6},{8,9},{9,8},{10,11... | collective-permute-start | bytes 98312 | tf_op jit(solution)/shard_map/ppermute | solution.py:490
  5.4 1.2 %copy-start.4 = (s32[4]{0:T(128)S(1)}, s32[4]{0:T(128)}, u32[]{:S(2)}) copy-start(s32[4]{0:T(128)} %param.9) | copy-start | bytes 52
  5.4 8.8 %collective-permute-start.1 = (s32[16,512]{1,0:T(8,128)S(1)}, s32[16,512]{1,0:T(8,128)S(1)}, u32[]{:S(2)}, u32[]{:S(2)}) collective-permute-start(s32[16,512]{1,0:T(8,128)S(1)} %get-tuple-element.29), channel_id=1, source_target_pairs={{0,16},{1,2},{2,1},{3,4},{4,3},{5,6},{6,5},{7,8},{8,7},{9,10},{10,... | collective-permute-start | bytes 98312 | tf_op jit(solution)/shard_map/ppermute | solution.py:491
  6.8 0.7 %copy-start.2 = (f32[2,4,5,17]{3,1,2,0:T(4,128)S(1)}, f32[2,4,5,17]{3,1,2,0:T(4,128)}, u32[]{:S(2)}) copy-start(f32[2,4,5,17]{3,1,2,0:T(4,128)} %param.7) | copy-start | bytes 8164
  8.8 8.7 %collective-permute-start = (f32[8,16,512]{2,1,0:T(8,128)S(1)}, f32[8,16,512]{2,1,0:T(8,128)S(1)}, u32[]{:S(2)}, u32[]{:S(2)}) collective-permute-start(f32[8,16,512]{2,1,0:T(8,128)S(1)} %get-tuple-element.17), channel_id=1, source_target_pairs={{0,16},{1,2},{2,1},{3,4},{4,3},{5,6},{6,5},{7,8},{8,7},{9,10},{10,... | collective-permute-start | bytes 786440 | tf_op jit(solution)/shard_map/ppermute | solution.py:492

commit v4 on v2

--- a/solution.py
+++ b/solution.py
@@ -168,7 +168,7 @@
     return [[[[pair[n] for pair in kind] for kind in field] for field in both] for n in range(2)]
 
 
-def crossline(lhs, first, second, masks, block):
+def crossline(lhs, first, second, masks, block, ready=None):
     wide = 2 * LANES
     width = first[0][0][0].shape[1]
     pieces = [[[], []], [[], []]]
@@ -180,6 +180,8 @@
         got = band_pick(found.pop(0), [m[:, at : at + wide] for m in masks], block)
         for part in range(2):
             pieces[i][part].append(got[part])
+        if ready is not None and at + wide == width:
+            ready(i, *[jnp.concatenate(p, axis=1) for p in pieces[i]])
 
     for n, (i, at) in enumerate(spots):
         windows = [
@@ -220,9 +222,9 @@
     return [rotate(field, cosine, sine) for field in fields]
 
 
-def put_done(done_ref, f, fields):
-    (sr, si), (qr, qi) = fields
-    done_ref[0, 0, f], done_ref[0, 1, f], done_ref[1, 0, f], done_ref[1, 1, f] = sr, si, qr, -qi
+def put_done(done_ref, f, i, real, imag):
+    done_ref[i, 0, f] = real
+    done_ref[i, 1, f] = -imag if i else imag
 
 
 def window_levels(ref, inner, outer, inner_at, block):
@@ -291,9 +293,9 @@
             save(mid_ref, f, ready[f, 3])
 
     def last_chain(f):
-        fields = yield from crossline(lhs_ref[f], *ordered(c == 1, ready[f, 3], ready[f, 4]), masks[1], block)
+        done = functools.partial(put_done, done_ref, f)
+        fields = yield from crossline(lhs_ref[f], *ordered(c == 1, ready[f, 3], ready[f, 4]), masks[1], block, done)
         acc_ref[2] += image_of(fields)
-        put_done(done_ref, f, fields)
 
     interleave([start_chain(f, slot) for f in range(freqs) for slot in range(3)], SKEW1)
     interleave([next_chain(f, slot) for f in range(freqs) for slot in range(2)], SKEW1)
@@ -368,11 +370,15 @@
         fields = yield from inline(lhs_ref[f], fields, lambda: level_masks(levt_ref[1], levels), block)
         outer = split_fields(fields)
         yield
-        fields = yield from crossline(lhs_ref[f], *ordered(c == 0, saved(mid_ref, f), outer), masks_near, block)
+
+        def done(i, real, imag):
+            put_done(done_ref, g, i, real, imag)
+            if last:
+                send(done_ref.at[i, :, g], out_ref.at[i, :, f, pl.ds(slow_row, block)])
+
+        last_pair = ordered(c == 0, saved(mid_ref, f), outer)
+        fields = yield from crossline(lhs_ref[f], *last_pair, masks_near, block, done)
         sum_ref[1] += image_of(fields)
-        put_done(done_ref, g, fields)
-        if last:
-            send(done_ref.at[:, :, g], out_ref.at[:, :, f, pl.ds(slow_row, block)])
 
     interleave([chain(g) for g in range(group)], SKEW)
     if last:
@@ -462,7 +468,7 @@
             args += [own_done, own_sum, *parts]
             outs = [waves.shape, (STEPS, rows, width)]
             scratch = [pltpu.VMEM(shape, F32) for shape in shapes] + scratch
-            scratch.append(pltpu.SemaphoreType.DMA((groups + group + 5,)))
+            scratch.append(pltpu.SemaphoreType.DMA((groups + 2 * group + 5,)))
         result = pl.pallas_call(
             functools.partial(second_kernel, g * group, g == 0, last),
             out_shape=[jax.ShapeDtypeStruct(shape, F32) for shape in outs],

time: 19.4 us -> 19.4 us (level)
  no operation moved by 1% of the time
where the time goes in v4:
time: 19.4 us; the launch traced here: 19.2 us
  Pallas kernels  9.11 us (47%)
  starting transfers between devices  4.29 us (22%)
  local copies, waits for them, and re-layouts  2.49 us (13%)
  waiting for transfers between devices  2.44 us (13%)
  between operations  0.75 us (4%)
    pallas_call x1, Pallas kernels, on_device(): pl.pallas_call(first_kernel, out_shape=[jax.ShapeDtypeStruct((2, 2, freqs...  5.08 us
    pallas_call x2, Pallas kernels, on_device(): pl.pallas_call(functools.partial(second_kernel, g * group, g == 0, last),...  4.03 us
    ppermute x1, starting transfers between devices, on_device(): slow = [lax.ppermute(side(waves, slow_row, 0, group), axes, across)]  1.86 us
    ppermute x1, waiting for transfers between devices, on_device(): lax.ppermute(lax.dynamic_slice_in_dim(marks, slow_row, block, axis=0), ax...  1.29 us
    ppermute x1, starting transfers between devices, on_device(): lax.ppermute(lax.dynamic_slice_in_dim(marks, slow_row, block, axis=0), ax...  1.2 us
    ppermute x1, waiting for transfers between devices, on_device(): lax.ppermute(side(cells, slow_row, g * group, (g + 1) * group), axes, acr...  1.15 us
    dynamic_slice x1, local copies, waits for them, and re-layouts, side(): cells = lax.dynamic_slice_in_dim(cells, start, block, axis=3)  1.11 us
    slice x2, local copies, waits for them, and re-layouts, side(): return cells[:, :, low:high].reshape(-1, block, width)  1.08 us
  transfers between devices with their start and end apart: 5, of which 2 were waited for; matrix products, arithmetic and copies ran while one was open for 7% of the time, Pallas kernels for 35%

profile of v4, /device:TPU:9, one launch (start us, length us, event | category | flops | bytes accessed | tf_op | source)
XLA Modules:
  0.0 19.2 jit_solution(10294061759981594096)
XLA Ops:
  0.6 0.0 copy-start
  0.7 1.1 %constant_dynamic-slice_fusion = f32[2,2,2,16,512]{4,3,2,1,0:T(8,128)S(1)} fusion(f32[2,2,4,32,512]{4,3,2,1,0:T(8,128)} %waves_ref.1, s32[]{:T(128)S(6)} %select_n.18), kind=kLoop, calls=%fused_computation | loop fusion | bytes 524292 | tf_op jit(solution)/shard_map/slice | solution.py:413
  1.7 1.9 %collective-permute-start.4 = (f32[8,16,512]{2,1,0:T(8,128)S(1)}, f32[8,16,512]{2,1,0:T(8,128)S(1)}, u32[]{:S(2)}, u32[]{:S(2)}) collective-permute-start(f32[8,16,512]{2,1,0:T(8,128)S(1)} %bitcast.4), channel_id=1, source_target_pairs={{0,16},{1,2},{2,1},{3,4},{4,3},{5,6},{6,5},{7,8},{8,7},{9,10},{10,... | collective-permute-start | bytes 786440 | tf_op jit(solution)/shard_map/ppermute | solution.py:426
  3.6 1.1 %constant_dynamic-slice_fusion.4 = f32[2,2,4,16,512]{4,3,2,1,0:T(8,128)S(1)} fusion(f32[2,2,4,32,512]{4,3,2,1,0:T(8,128)} %waves_ref.1, s32[]{:T(128)S(6)} %select_n.17), kind=kLoop, calls=%fused_computation.4 | loop fusion | bytes 1048580 | tf_op jit(solution)/shard_map/dynamic_slice | solution.py:412
  4.7 0.1 collective-permute-start.2
  4.8 0.0 copy-done.1
  4.8 0.5 %collective-permute-start.3 = (s32[16,512]{1,0:T(8,128)S(1)}, s32[16,512]{1,0:T(8,128)S(1)}, u32[]{:S(2)}, u32[]{:S(2)}) collective-permute-start(s32[16,512]{1,0:T(8,128)S(1)} %get-tuple-element.22), channel_id=1, source_target_pairs={{0,1},{1,0},{2,3},{3,2},{4,5},{5,4},{6,7},{7,6},{8,9},{9,8},{10,11... | collective-permute-start | bytes 98312 | tf_op jit(solution)/shard_map/ppermute | solution.py:430
  5.4 1.2 %collective-permute-start.1 = (s32[16,512]{1,0:T(8,128)S(1)}, s32[16,512]{1,0:T(8,128)S(1)}, u32[]{:S(2)}, u32[]{:S(2)}) collective-permute-start(s32[16,512]{1,0:T(8,128)S(1)} %get-tuple-element.23), channel_id=1, source_target_pairs={{0,16},{1,2},{2,1},{3,4},{4,3},{5,6},{6,5},{7,8},{8,7},{9,10},{10,... | collective-permute-start | bytes 98312 | tf_op jit(solution)/shard_map/ppermute | solution.py:431
  6.6 0.0 copy-done
  6.6 0.0 copy-start.2
  6.6 0.6 %collective-permute-start = (f32[8,16,512]{2,1,0:T(8,128)S(1)}, f32[8,16,512]{2,1,0:T(8,128)S(1)}, u32[]{:S(2)}, u32[]{:S(2)}) collective-permute-start(f32[8,16,512]{2,1,0:T(8,128)S(1)} %bitcast.5), channel_id=1, source_target_pairs={{0,16},{1,2},{2,1},{3,4},{4,3},{5,6},{6,5},{7,8},{8,7},{9,10},{10,... | collective-permute-start | bytes 786440 | tf_op jit(solution)/shard_map/ppermute | solution.py:433
  7.2 0.0 copy-done.4
  7.2 0.0 copy-done.3
  7.3 0.1 reshape.21
  7.4 0.1 reshape.22
  7.5 0.1 pad_maximum_fusion.meta_ref
  7.6 0.0 collective-permute-done.3.halo_ref
  7.6 0.0 collective-permute-done.2.fast_ref
  7.6 5.1 %own_rows.1 = (f32[2,2,4,16,512]{4,3,2,1,0:T(8,128)S(1)}, f32[3,16,512]{2,1,0:T(8,128)S(1)}, bf16[4,2,2,2,16,512]{5,4,3,2,1,0:T(8,128)(2,1)S(1)}, bf16[4,2,2,2,1...) custom-call(f32[44]{0:T(128)S(1)} %pad_maximum_fusion.meta_ref, ...), custom_call_target="tpu_custom_call" | custom-call | flops 4026531840 | bytes 8388608 | tf_op jit(solution)/shard_map/own_rows/pallas_call | solution.py:439
  12.7 1.3 %collective-permute-done.1.halo_ref = s32[16,512]{1,0:T(8,128)S(1)} collective-permute-done((s32[16,512]{1,0:T(8,128)S(1)}, s32[16,512]{1,0:T(8,128)S(1)}, u32[]{:S(2)}, u32[]{:S(2)}) %collective-permute-start.1) | collective-permute-done | bytes 32800 | tf_op jit(solution)/shard_map/ppermute | solution.py:431
  14.0 0.0 collective-permute-done.4.slow_ref
  14.0 1.7 %edge_rows_0.1 = (f32[2,16,512]{2,1,0:T(8,128)S(1)}, f32[2,2,2,16,512]{4,3,2,1,0:T(8,128)S(1)}) custom-call(f32[8,16,512]{2,1,0:T(8,128)S(1)} %collective-permute-done.4.slow_ref, s32[16,512]{1,0:T(8,128)S(1)} %collective-permute-done.1.halo_ref, s32[32,512]{1,0:T(8,128)S(1)} %copy-done.1, bf16[4,160,256]{2,1,0:T(8,128)(2,1)S(1)} %get-tuple-element.14.lhs_ref, ...), custom_call_target="tpu_custom_call" | custom-call | flops 1006632960 | bytes 4194304 | tf_op jit(solution)/shard_map/edge_rows_0/pallas_call | solution.py:472
  15.6 1.1 %collective-permute-done.slow_ref = f32[8,16,512]{2,1,0:T(8,128)S(1)} collective-permute-done((f32[8,16,512]{2,1,0:T(8,128)S(1)}, f32[8,16,512]{2,1,0:T(8,128)S(1)}, u32[]{:S(2)}, u32[]{:S(2)}) %collective-permute-start) | collective-permute-done | bytes 262176 | tf_op jit(solution)/shard_map/ppermute | solution.py:433
  16.8 2.4 %edge_rows_1.1 = (f32[2,2,4,32,512]{4,3,2,1,0:T(8,128)}, f32[2,32,512]{2,1,0:T(8,128)}) custom-call(f32[8,16,512]{2,1,0:T(8,128)S(1)} %collective-permute-done.slow_ref, s32[16,512]{1,0:T(8,128)S(1)} %collective-permute-done.1.halo_ref, s32[32,512]{1,0:T(8,128)S(1)} %copy-done.1, bf16[4,160,256]{2,1,0:T(8,128)(2,1)S(1)} %get-tuple-element.14.lhs_ref, ...), custom_call_target="tpu_custom_call" | custom-call | flops 1006632960 | bytes 4194304 | tf_op jit(solution)/shard_map/edge_rows_1/pallas_call | solution.py:472
  (9 shorter events, 0.1 us)
Async XLA Ops:
  0.6 5.9 %copy-start = (f32[2,2,4,32,512]{4,3,2,1,0:T(8,128)S(1)}, f32[2,2,4,32,512]{4,3,2,1,0:T(8,128)}, u32[]{:S(2)}) copy-start(f32[2,2,4,32,512]{4,3,2,1,0:T(8,128)} %waves_ref.1) | copy-start | bytes 3145732
  1.7 12.2 %collective-permute-start.4 = (f32[8,16,512]{2,1,0:T(8,128)S(1)}, f32[8,16,512]{2,1,0:T(8,128)S(1)}, u32[]{:S(2)}, u32[]{:S(2)}) collective-permute-start(f32[8,16,512]{2,1,0:T(8,128)S(1)} %bitcast.4), channel_id=1, source_target_pairs={{0,16},{1,2},{2,1},{3,4},{4,3},{5,6},{6,5},{7,8},{8,7},{9,10},{10,... | collective-permute-start | bytes 786440 | tf_op jit(solution)/shard_map/ppermute | solution.py:426
  3.6 1.2 %copy-start.1 = (s32[32,512]{1,0:T(8,128)S(1)}, s32[32,512]{1,0:T(8,128)}, u32[]{:S(2)}) copy-start(s32[32,512]{1,0:T(8,128)} %lev_ref.5) | copy-start | bytes 196612
  4.7 2.9 %collective-permute-start.2 = (f32[16,16,512]{2,1,0:T(8,128)S(1)}, f32[16,16,512]{2,1,0:T(8,128)S(1)}, u32[]{:S(2)}, u32[]{:S(2)}) collective-permute-start(f32[16,16,512]{2,1,0:T(8,128)S(1)} %bitcast.3), channel_id=1, source_target_pairs={{0,1},{1,0},{2,3},{3,2},{4,5},{5,4},{6,7},{7,6},{8,9},{9,8},{10,11... | collective-permute-start | bytes 1572872 | tf_op jit(solution)/shard_map/ppermute | solution.py:428
  4.8 2.8 %collective-permute-start.3 = (s32[16,512]{1,0:T(8,128)S(1)}, s32[16,512]{1,0:T(8,128)S(1)}, u32[]{:S(2)}, u32[]{:S(2)}) collective-permute-start(s32[16,512]{1,0:T(8,128)S(1)} %get-tuple-element.22), channel_id=1, source_target_pairs={{0,1},{1,0},{2,3},{3,2},{4,5},{5,4},{6,7},{7,6},{8,9},{9,8},{10,11... | collective-permute-start | bytes 98312 | tf_op jit(solution)/shard_map/ppermute | solution.py:430
  5.4 8.6 %collective-permute-start.1 = (s32[16,512]{1,0:T(8,128)S(1)}, s32[16,512]{1,0:T(8,128)S(1)}, u32[]{:S(2)}, u32[]{:S(2)}) collective-permute-start(s32[16,512]{1,0:T(8,128)S(1)} %get-tuple-element.23), channel_id=1, source_target_pairs={{0,16},{1,2},{2,1},{3,4},{4,3},{5,6},{6,5},{7,8},{8,7},{9,10},{10,... | collective-permute-start | bytes 98312 | tf_op jit(solution)/shard_map/ppermute | solution.py:431
  6.6 0.7 %copy-start.4 = (s32[4]{0:T(128)S(1)}, s32[4]{0:T(128)}, u32[]{:S(2)}) copy-start(s32[4]{0:T(128)} %param.9) | copy-start | bytes 52
  6.6 0.7 %copy-start.3 = (f32[4,5]{1,0:T(4,128)S(1)}, f32[4,5]{1,0:T(4,128)}, u32[]{:S(2)}) copy-start(f32[4,5]{1,0:T(4,128)} %param.8) | copy-start | bytes 244
  6.6 1.0 %copy-start.2 = (f32[2,4,5,17]{3,1,2,0:T(4,128)S(1)}, f32[2,4,5,17]{3,1,2,0:T(4,128)}, u32[]{:S(2)}) copy-start(f32[2,4,5,17]{3,1,2,0:T(4,128)} %param.7) | copy-start | bytes 8164
  6.6 10.2 %collective-permute-start = (f32[8,16,512]{2,1,0:T(8,128)S(1)}, f32[8,16,512]{2,1,0:T(8,128)S(1)}, u32[]{:S(2)}, u32[]{:S(2)}) collective-permute-start(f32[8,16,512]{2,1,0:T(8,128)S(1)} %bitcast.5), channel_id=1, source_target_pairs={{0,16},{1,2},{2,1},{3,4},{4,3},{5,6},{6,5},{7,8},{8,7},{9,10},{10,... | collective-permute-start | bytes 786440 | tf_op jit(solution)/shard_map/ppermute | solution.py:433

commit v5 on v2

--- a/solution.py
+++ b/solution.py
@@ -385,7 +385,7 @@
 SMEM = pl.BlockSpec(memory_space=pltpu.SMEM)
 ANY = pl.BlockSpec(memory_space=pl.ANY)
 LIMIT = 48 * 1024 * 1024
-SKEW = 3
+SKEW = 4
 SKEW1 = 2
 LAG = 1
 GROUPS = 2

time: 19.4 us -> 19.4 us (level)
  no operation moved by 1% of the time
where the time goes in v5:
time: 19.4 us; the launch traced here: 19.2 us
  Pallas kernels  9.11 us (47%)
  starting transfers between devices  4.29 us (22%)
  local copies, waits for them, and re-layouts  2.49 us (13%)
  waiting for transfers between devices  2.45 us (13%)
  between operations  0.75 us (4%)
    pallas_call x1, Pallas kernels, on_device(): pl.pallas_call(first_kernel, out_shape=[jax.ShapeDtypeStruct((2, 2, freqs...  5.08 us
    pallas_call x2, Pallas kernels, on_device(): pl.pallas_call(functools.partial(second_kernel, g * group, g == 0, last),...  4.03 us
    ppermute x1, starting transfers between devices, on_device(): slow = [lax.ppermute(side(waves, slow_row, 0, group), axes, across)]  1.86 us
    ppermute x1, waiting for transfers between devices, on_device(): lax.ppermute(lax.dynamic_slice_in_dim(marks, slow_row, block, axis=0), ax...  1.29 us
    ppermute x1, starting transfers between devices, on_device(): lax.ppermute(lax.dynamic_slice_in_dim(marks, slow_row, block, axis=0), ax...  1.2 us
    ppermute x1, waiting for transfers between devices, on_device(): lax.ppermute(side(cells, slow_row, g * group, (g + 1) * group), axes, acr...  1.16 us
    dynamic_slice x1, local copies, waits for them, and re-layouts, side(): cells = lax.dynamic_slice_in_dim(cells, start, block, axis=3)  1.11 us
    slice x2, local copies, waits for them, and re-layouts, side(): return cells[:, :, low:high].reshape(-1, block, width)  1.08 us
  transfers between devices with their start and end apart: 5, of which 2 were waited for; matrix products, arithmetic and copies ran while one was open for 7% of the time, Pallas kernels for 35%

profile of v5, /device:TPU:9, one launch (start us, length us, event | category | flops | bytes accessed | tf_op | source)
XLA Modules:
  0.0 19.2 jit_solution(13419526308889213133)
XLA Ops:
  0.6 0.0 copy-start
  0.7 1.1 %constant_dynamic-slice_fusion = f32[2,2,2,16,512]{4,3,2,1,0:T(8,128)S(1)} fusion(f32[2,2,4,32,512]{4,3,2,1,0:T(8,128)} %waves_ref.1, s32[]{:T(128)S(6)} %select_n.18), kind=kLoop, calls=%fused_computation | loop fusion | bytes 524292 | tf_op jit(solution)/shard_map/slice | solution.py:407
  1.7 1.9 %collective-permute-start.4 = (f32[8,16,512]{2,1,0:T(8,128)S(1)}, f32[8,16,512]{2,1,0:T(8,128)S(1)}, u32[]{:S(2)}, u32[]{:S(2)}) collective-permute-start(f32[8,16,512]{2,1,0:T(8,128)S(1)} %bitcast.4), channel_id=1, source_target_pairs={{0,16},{1,2},{2,1},{3,4},{4,3},{5,6},{6,5},{7,8},{8,7},{9,10},{10,... | collective-permute-start | bytes 786440 | tf_op jit(solution)/shard_map/ppermute | solution.py:420
  3.6 1.1 %constant_dynamic-slice_fusion.4 = f32[2,2,4,16,512]{4,3,2,1,0:T(8,128)S(1)} fusion(f32[2,2,4,32,512]{4,3,2,1,0:T(8,128)} %waves_ref.1, s32[]{:T(128)S(6)} %select_n.17), kind=kLoop, calls=%fused_computation.4 | loop fusion | bytes 1048580 | tf_op jit(solution)/shard_map/dynamic_slice | solution.py:406
  4.7 0.1 collective-permute-start.2
  4.8 0.0 copy-done.1
  4.8 0.5 %collective-permute-start.3 = (s32[16,512]{1,0:T(8,128)S(1)}, s32[16,512]{1,0:T(8,128)S(1)}, u32[]{:S(2)}, u32[]{:S(2)}) collective-permute-start(s32[16,512]{1,0:T(8,128)S(1)} %get-tuple-element.22), channel_id=1, source_target_pairs={{0,1},{1,0},{2,3},{3,2},{4,5},{5,4},{6,7},{7,6},{8,9},{9,8},{10,11... | collective-permute-start | bytes 98312 | tf_op jit(solution)/shard_map/ppermute | solution.py:424
  5.4 1.2 %collective-permute-start.1 = (s32[16,512]{1,0:T(8,128)S(1)}, s32[16,512]{1,0:T(8,128)S(1)}, u32[]{:S(2)}, u32[]{:S(2)}) collective-permute-start(s32[16,512]{1,0:T(8,128)S(1)} %get-tuple-element.23), channel_id=1, source_target_pairs={{0,16},{1,2},{2,1},{3,4},{4,3},{5,6},{6,5},{7,8},{8,7},{9,10},{10,... | collective-permute-start | bytes 98312 | tf_op jit(solution)/shard_map/ppermute | solution.py:425
  6.6 0.0 copy-done
  6.6 0.0 copy-start.2
  6.6 0.6 %collective-permute-start = (f32[8,16,512]{2,1,0:T(8,128)S(1)}, f32[8,16,512]{2,1,0:T(8,128)S(1)}, u32[]{:S(2)}, u32[]{:S(2)}) collective-permute-start(f32[8,16,512]{2,1,0:T(8,128)S(1)} %bitcast.5), channel_id=1, source_target_pairs={{0,16},{1,2},{2,1},{3,4},{4,3},{5,6},{6,5},{7,8},{8,7},{9,10},{10,... | collective-permute-start | bytes 786440 | tf_op jit(solution)/shard_map/ppermute | solution.py:427
  7.2 0.0 copy-done.4
  7.2 0.0 copy-done.3
  7.3 0.1 reshape.21
  7.4 0.1 reshape.22
  7.5 0.1 pad_maximum_fusion.meta_ref
  7.6 0.0 collective-permute-done.3.halo_ref
  7.6 0.0 collective-permute-done.2.fast_ref
  7.6 5.1 %own_rows.1 = (f32[2,2,4,16,512]{4,3,2,1,0:T(8,128)S(1)}, f32[3,16,512]{2,1,0:T(8,128)S(1)}, bf16[4,2,2,2,16,512]{5,4,3,2,1,0:T(8,128)(2,1)S(1)}, bf16[4,2,2,2,1...) custom-call(f32[44]{0:T(128)S(1)} %pad_maximum_fusion.meta_ref, ...), custom_call_target="tpu_custom_call" | custom-call | flops 4026531840 | bytes 8388608 | tf_op jit(solution)/shard_map/own_rows/pallas_call | solution.py:433
  12.7 1.3 %collective-permute-done.1.halo_ref = s32[16,512]{1,0:T(8,128)S(1)} collective-permute-done((s32[16,512]{1,0:T(8,128)S(1)}, s32[16,512]{1,0:T(8,128)S(1)}, u32[]{:S(2)}, u32[]{:S(2)}) %collective-permute-start.1) | collective-permute-done | bytes 32800 | tf_op jit(solution)/shard_map/ppermute | solution.py:425
  14.0 0.0 collective-permute-done.4.slow_ref
  14.0 1.6 %edge_rows_0.1 = (f32[2,16,512]{2,1,0:T(8,128)S(1)}, f32[2,2,2,16,512]{4,3,2,1,0:T(8,128)S(1)}) custom-call(f32[8,16,512]{2,1,0:T(8,128)S(1)} %collective-permute-done.4.slow_ref, s32[16,512]{1,0:T(8,128)S(1)} %collective-permute-done.1.halo_ref, s32[32,512]{1,0:T(8,128)S(1)} %copy-done.1, bf16[4,160,256]{2,1,0:T(8,128)(2,1)S(1)} %get-tuple-element.14.lhs_ref, ...), custom_call_target="tpu_custom_call" | custom-call | flops 1006632960 | bytes 4194304 | tf_op jit(solution)/shard_map/edge_rows_0/pallas_call | solution.py:466
  15.6 1.2 %collective-permute-done.slow_ref = f32[8,16,512]{2,1,0:T(8,128)S(1)} collective-permute-done((f32[8,16,512]{2,1,0:T(8,128)S(1)}, f32[8,16,512]{2,1,0:T(8,128)S(1)}, u32[]{:S(2)}, u32[]{:S(2)}) %collective-permute-start) | collective-permute-done | bytes 262176 | tf_op jit(solution)/shard_map/ppermute | solution.py:427
  16.8 2.4 %edge_rows_1.1 = (f32[2,2,4,32,512]{4,3,2,1,0:T(8,128)}, f32[2,32,512]{2,1,0:T(8,128)}) custom-call(f32[8,16,512]{2,1,0:T(8,128)S(1)} %collective-permute-done.slow_ref, s32[16,512]{1,0:T(8,128)S(1)} %collective-permute-done.1.halo_ref, s32[32,512]{1,0:T(8,128)S(1)} %copy-done.1, bf16[4,160,256]{2,1,0:T(8,128)(2,1)S(1)} %get-tuple-element.14.lhs_ref, ...), custom_call_target="tpu_custom_call" | custom-call | flops 1006632960 | bytes 4194304 | tf_op jit(solution)/shard_map/edge_rows_1/pallas_call | solution.py:466
  (9 shorter events, 0.1 us)
Async XLA Ops:
  0.6 5.9 %copy-start = (f32[2,2,4,32,512]{4,3,2,1,0:T(8,128)S(1)}, f32[2,2,4,32,512]{4,3,2,1,0:T(8,128)}, u32[]{:S(2)}) copy-start(f32[2,2,4,32,512]{4,3,2,1,0:T(8,128)} %waves_ref.1) | copy-start | bytes 3145732
  1.7 12.2 %collective-permute-start.4 = (f32[8,16,512]{2,1,0:T(8,128)S(1)}, f32[8,16,512]{2,1,0:T(8,128)S(1)}, u32[]{:S(2)}, u32[]{:S(2)}) collective-permute-start(f32[8,16,512]{2,1,0:T(8,128)S(1)} %bitcast.4), channel_id=1, source_target_pairs={{0,16},{1,2},{2,1},{3,4},{4,3},{5,6},{6,5},{7,8},{8,7},{9,10},{10,... | collective-permute-start | bytes 786440 | tf_op jit(solution)/shard_map/ppermute | solution.py:420
  3.6 1.2 %copy-start.1 = (s32[32,512]{1,0:T(8,128)S(1)}, s32[32,512]{1,0:T(8,128)}, u32[]{:S(2)}) copy-start(s32[32,512]{1,0:T(8,128)} %lev_ref.5) | copy-start | bytes 196612
  4.7 2.9 %collective-permute-start.2 = (f32[16,16,512]{2,1,0:T(8,128)S(1)}, f32[16,16,512]{2,1,0:T(8,128)S(1)}, u32[]{:S(2)}, u32[]{:S(2)}) collective-permute-start(f32[16,16,512]{2,1,0:T(8,128)S(1)} %bitcast.3), channel_id=1, source_target_pairs={{0,1},{1,0},{2,3},{3,2},{4,5},{5,4},{6,7},{7,6},{8,9},{9,8},{10,11... | collective-permute-start | bytes 1572872 | tf_op jit(solution)/shard_map/ppermute | solution.py:422
  4.8 2.8 %collective-permute-start.3 = (s32[16,512]{1,0:T(8,128)S(1)}, s32[16,512]{1,0:T(8,128)S(1)}, u32[]{:S(2)}, u32[]{:S(2)}) collective-permute-start(s32[16,512]{1,0:T(8,128)S(1)} %get-tuple-element.22), channel_id=1, source_target_pairs={{0,1},{1,0},{2,3},{3,2},{4,5},{5,4},{6,7},{7,6},{8,9},{9,8},{10,11... | collective-permute-start | bytes 98312 | tf_op jit(solution)/shard_map/ppermute | solution.py:424
  5.4 8.6 %collective-permute-start.1 = (s32[16,512]{1,0:T(8,128)S(1)}, s32[16,512]{1,0:T(8,128)S(1)}, u32[]{:S(2)}, u32[]{:S(2)}) collective-permute-start(s32[16,512]{1,0:T(8,128)S(1)} %get-tuple-element.23), channel_id=1, source_target_pairs={{0,16},{1,2},{2,1},{3,4},{4,3},{5,6},{6,5},{7,8},{8,7},{9,10},{10,... | collective-permute-start | bytes 98312 | tf_op jit(solution)/shard_map/ppermute | solution.py:425
  6.6 0.7 %copy-start.4 = (s32[4]{0:T(128)S(1)}, s32[4]{0:T(128)}, u32[]{:S(2)}) copy-start(s32[4]{0:T(128)} %param.9) | copy-start | bytes 52
  6.6 0.7 %copy-start.3 = (f32[4,5]{1,0:T(4,128)S(1)}, f32[4,5]{1,0:T(4,128)}, u32[]{:S(2)}) copy-start(f32[4,5]{1,0:T(4,128)} %param.8) | copy-start | bytes 244
  6.6 1.0 %copy-start.2 = (f32[2,4,5,17]{3,1,2,0:T(4,128)S(1)}, f32[2,4,5,17]{3,1,2,0:T(4,128)}, u32[]{:S(2)}) copy-start(f32[2,4,5,17]{3,1,2,0:T(4,128)} %param.7) | copy-start | bytes 8164
  6.6 10.2 %collective-permute-start = (f32[8,16,512]{2,1,0:T(8,128)S(1)}, f32[8,16,512]{2,1,0:T(8,128)S(1)}, u32[]{:S(2)}, u32[]{:S(2)}) collective-permute-start(f32[8,16,512]{2,1,0:T(8,128)S(1)} %bitcast.5), channel_id=1, source_target_pairs={{0,16},{1,2},{2,1},{3,4},{4,3},{5,6},{6,5},{7,8},{8,7},{9,10},{10,... | collective-permute-start | bytes 786440 | tf_op jit(solution)/shard_map/ppermute | solution.py:427
